TPU v7x, 256 devices: a whole 4x4x8 slice. The times are simulated.
256 devices in a mesh: dp: 8 (over x, core), ctx: 32 (over z, y).
Axes of the slice: x: 4, y: 4, z: 8, core: 2. Of those that a mesh axis runs over, the one named last changes fastest.
Arguments:
- hidden: bfloat16 [8, 4096, 8192], P('dp', 'ctx'), may hold values from -6 to 6
- queries: bfloat16 [8, 4096, 4096], P('dp', 'ctx'), may hold values from -48 to 48
- keys: bfloat16 [8, 4096, 512], P('dp', 'ctx'), may hold values from -5 to 5
- adapter_down_factor: bfloat16 [8192, 64], replicated, may hold values from -0.0625 to 0.0625
- adapter_up_factor: bfloat16 [64, 512], replicated, may hold values from -0.75 to 0.75
- down_direction: bfloat16 [8192, 64], replicated, may hold values from -0.59765625 to 0.59765625
- up_direction: bfloat16 [64, 512], replicated, may hold values from -6 to 6
- trajectory_window_index: int32 [8], P('dp'), may hold values from 0 to 3
- lengths: int32 [8], P('dp'), may hold values from 1024 to 17407, as said below
Outputs:
- fisher_down: float32 [8192, 64], P('ctx')
- fisher_up: float32 [64, 512], P(None, 'ctx')
- curvature: float32 [], replicated
Inputs may be any that keep to these rules, and one draw needn't show every extreme that they name: lengths[b] - 4096 * trajectory_window_index[b] lies between a quarter and five quarters of 4096.
All inputs are finite; a program needn't handle non-finite values.
Results may differ from a plain program's by a relative error of at most 0.0059.
Values may be sent and summed in bfloat16 or wider, within the bound.
A program may use at most 64 MiB of HBM per device.

v0:
```python
import math

import jax
import jax.numpy as jnp
from jax import lax
from jax.sharding import PartitionSpec as P

HEAD_WIDTH = 128
GROUP = 8


def rotate(values, positions, head_count, head_size):
    half_size = head_size // 2
    inv_freq = jnp.exp(
        jnp.arange(half_size, dtype=jnp.float32) * (-2.0 * math.log(1000000.0) / head_size)
    )
    angles = positions.astype(jnp.float32)[..., None] * inv_freq
    cosine = jnp.cos(angles)[..., None, :]
    sine_part = jnp.sin(angles)[..., None, :]
    lead_shape = values.shape[:-1]
    as_heads = values.astype(jnp.float32).reshape(lead_shape + (head_count, head_size))
    lower_half = as_heads[..., :half_size]
    upper_half = as_heads[..., half_size:]
    turned = jnp.concatenate(
        [
            lower_half * cosine - upper_half * sine_part,
            upper_half * cosine + lower_half * sine_part,
        ],
        axis=-1,
    )
    return turned.reshape(values.shape).astype(jnp.bfloat16)


def attend(query_rows, key_rows, tangent_rows, valid_rows):
    span_len = query_rows.shape[0]
    block_rows = math.gcd(span_len, 512)
    score_scale = 1.0 / math.sqrt(query_rows.shape[1])
    columns = jnp.arange(span_len, dtype=jnp.int32)

    def block_step(block_index, carry_in):
        grad_sum, curvature_sum = carry_in
        row_start = block_index * block_rows
        query_block = lax.dynamic_slice_in_dim(query_rows, row_start, block_rows, 0)
        scores = (
            jnp.einsum("qd,kd->qk", query_block, key_rows, preferred_element_type=jnp.float32)
            * score_scale
        )
        causal = columns[None, :] <= (row_start + jnp.arange(block_rows, dtype=jnp.int32))[:, None]
        scores = jnp.where(causal, scores, -jnp.inf)
        row_max = jnp.max(scores, axis=1, keepdims=True)
        weights = jnp.exp(scores - row_max)
        probs_bf = (weights / jnp.sum(weights, axis=1, keepdims=True)).astype(jnp.bfloat16)
        out_tangent = jnp.dot(probs_bf, tangent_rows, preferred_element_type=jnp.float32)
        keep_rows = lax.dynamic_slice_in_dim(valid_rows, row_start, block_rows, 0)[:, None]
        cotangent = (out_tangent * keep_rows).astype(jnp.bfloat16)
        grad_sum = grad_sum + jnp.einsum(
            "qk,qd->kd", probs_bf, cotangent, preferred_element_type=jnp.float32
        )
        curvature_sum = curvature_sum + jnp.sum(keep_rows * out_tangent * out_tangent)
        return (grad_sum, curvature_sum)

    init_carry = (
        jnp.zeros((span_len, query_rows.shape[1]), jnp.float32),
        jnp.zeros((), jnp.float32),
    )
    grad_sum, curvature_sum = lax.fori_loop(0, span_len // block_rows, block_step, init_carry)
    return (grad_sum.astype(jnp.bfloat16), curvature_sum)


def body(
    hidden,
    queries,
    keys,
    adapter_down_factor,
    adapter_up_factor,
    down_direction,
    up_direction,
    trajectory_window_index,
    lengths,
):
    seq_len = hidden.shape[1]
    ctx_count = lax.axis_size("ctx")
    span_len = seq_len * ctx_count
    kv_heads = keys.shape[2] // HEAD_WIDTH
    head_count = kv_heads * GROUP
    ctx_place = lax.axis_index("ctx")
    local_pos = (
        trajectory_window_index[:, None] * span_len
        + ctx_place * seq_len
        + jnp.arange(seq_len, dtype=jnp.int32)[None, :]
    )
    rot_query = rotate(queries, local_pos, head_count, HEAD_WIDTH)
    rot_keys = rotate(keys, local_pos, kv_heads, HEAD_WIDTH)
    down_activation = jnp.dot(
        hidden[0], adapter_down_factor, preferred_element_type=jnp.float32
    ).astype(jnp.bfloat16)
    down_direction_rows = jnp.dot(
        hidden[0], down_direction, preferred_element_type=jnp.float32
    ).astype(jnp.bfloat16)
    local_count = jnp.sum((local_pos < lengths[:, None]).astype(jnp.float32))
    total_count = lax.psum(local_count, ("dp", "ctx"))

    def copy_heads(per_kv):
        return jnp.repeat(per_kv.reshape(1, seq_len, kv_heads, HEAD_WIDTH), GROUP, axis=2).reshape(
            1, seq_len, head_count * HEAD_WIDTH
        )

    value_direction = (
        jnp.dot(down_direction_rows, adapter_up_factor, preferred_element_type=jnp.float32)
        + jnp.dot(down_activation, up_direction, preferred_element_type=jnp.float32)
    ).astype(jnp.bfloat16)
    own_query, own_keys, own_tangent = (
        lax.all_to_all(rot_query, "ctx", split_axis=2, concat_axis=1, tiled=True),
        lax.all_to_all(copy_heads(rot_keys), "ctx", split_axis=2, concat_axis=1, tiled=True),
        lax.all_to_all(
            copy_heads(value_direction[None]), "ctx", split_axis=2, concat_axis=1, tiled=True
        ),
    )
    span_pos = trajectory_window_index[0] * span_len + jnp.arange(span_len, dtype=jnp.int32)
    valid_all = (span_pos < lengths[0]).astype(jnp.float32)
    cols = slice(0, HEAD_WIDTH)
    grad_piece, curv_piece = attend(
        own_query[0, :, cols], own_keys[0, :, cols], own_tangent[0, :, cols], valid_all
    )
    grad_rows = grad_piece[None]
    returned = lax.all_to_all(grad_rows, "ctx", split_axis=1, concat_axis=2, tiled=True)
    value_gradient = jnp.sum(
        returned.reshape(seq_len, kv_heads, GROUP, HEAD_WIDTH).astype(jnp.float32), axis=2
    )
    value_gradient = value_gradient.reshape(seq_len, kv_heads * HEAD_WIDTH).astype(jnp.bfloat16)
    mixed_rank_rows = jnp.einsum(
        "zf,sf->zs", value_gradient, adapter_up_factor, preferred_element_type=jnp.float32
    ).astype(jnp.bfloat16)
    down_part = jnp.einsum(
        "td,tr->dr", hidden[0], mixed_rank_rows, preferred_element_type=jnp.float32
    )
    up_part = jnp.einsum(
        "tr,tc->rc", down_activation, value_gradient, preferred_element_type=jnp.float32
    )
    down_rows, up_cols_sum = (
        lax.psum_scatter(down_part, "ctx", scatter_dimension=0, tiled=True),
        lax.psum_scatter(up_part, "ctx", scatter_dimension=1, tiled=True),
    )
    down_own, up_own = lax.psum((down_rows, up_cols_sum), "dp")
    curv_total = lax.psum(curv_piece, ("dp", "ctx"))
    tangent_sq = jnp.sum(jnp.square(down_direction.astype(jnp.float32))) + jnp.sum(
        jnp.square(up_direction.astype(jnp.float32))
    )
    rescale = tangent_sq / (curv_total + 1e-06)
    return (down_own * rescale, up_own * rescale, curv_total / total_count)


def solution(mesh):
    placed = (
        P("dp", "ctx", None),
        P("dp", "ctx", None),
        P("dp", "ctx", None),
        P(),
        P(),
        P(),
        P(),
        P("dp"),
        P("dp"),
    )
    return jax.shard_map(
        body,
        mesh=mesh,
        in_specs=placed,
        out_specs=(P("ctx", None), P(None, "ctx"), P()),
        check_vma=False,
    )
```

profile of v0, /device:TPU:1, one launch (start us, length us, event | category | flops | bytes accessed | tf_op | source)
XLA Modules:
  0.0 915.7 jit_solution(7118917963953177328)
XLA Ops:
  12.8 17.1 %copy.73 = bf16[1,128,4096]{1,0,2:T(2,128)(2,1)} copy(bf16[1,128,4096]{1,2,0:T(8,128)(2,1)S(1)} %bitcast.98) | data formatting | bytes 2097152 | tf_op jit(solution)/shard_map/convert_element_type | solution.py:31
  30.4 23.5 %reduce.1 = bf16[4096,128]{1,0:T(8,128)(2,1)S(1)} reduce(bf16[4096,1,128]{2,1,0:T(2,128)(2,1)} %bitcast.94, bf16[]{:T(256)} %broadcast.113), dimensions={1}, to_apply=%bitcast.78.reduce_sub_computation | reduce | bytes 2097154
  55.0 12.2 %all-to-all-start = ((bf16[32,2,8192]{2,1,0:T(2,128)(2,1)}), bf16[32,2,8192]{2,1,0:T(2,128)(2,1)S(1)}, u32[]{:S(2)}, u32[]{:S(2)}) async-start(bf16[32,2,8192]{2,1,0:T(2,128)(2,1)} %reshape.185), calls=%async_computation | async-start | bytes 2097152 | tf_op jit(solution)/shard_map/all_to_all | solution.py:113
  68.5 17.1 %copy.72 = bf16[1,128,4096]{1,0,2:T(2,128)(2,1)} copy(bf16[1,128,4096]{1,2,0:T(8,128)(2,1)S(1)} %bitcast.100) | data formatting | bytes 2097152 | tf_op jit(solution)/shard_map/broadcast_in_dim | solution.py:104
  85.6 24.4 %reduce.2 = bf16[4096,128]{1,0:T(8,128)(2,1)} reduce(bf16[4096,1,128]{2,1,0:T(2,128)(2,1)} %bitcast.96, bf16[]{:T(256)} %broadcast.113), dimensions={1}, to_apply=%bitcast.77.reduce_sub_computation | reduce | bytes 2097154
  112.2 9.7 %all-to-all-start.1 = ((bf16[32,2,8192]{2,1,0:T(2,128)(2,1)}), bf16[32,2,8192]{2,1,0:T(2,128)(2,1)}, u32[]{:S(2)}, u32[]{:S(2)}) async-start(bf16[32,2,8192]{2,1,0:T(2,128)(2,1)} %reshape.187), calls=%async_computation.1 | async-start | bytes 2097152 | tf_op jit(solution)/shard_map/all_to_all | solution.py:114
  127.7 17.1 %copy.71 = bf16[1,128,4096]{1,0,2:T(2,128)(2,1)} copy(bf16[1,128,4096]{1,2,0:T(8,128)(2,1)S(1)} %bitcast.101) | data formatting | bytes 2097152 | tf_op jit(solution)/shard_map/broadcast_in_dim | solution.py:104
  144.8 24.5 %reduce.3 = bf16[4096,128]{1,0:T(8,128)(2,1)} reduce(bf16[4096,1,128]{2,1,0:T(2,128)(2,1)} %bitcast.97, bf16[]{:T(256)} %broadcast.113), dimensions={1}, to_apply=%bitcast.76.reduce_sub_computation | reduce | bytes 2097154
  171.4 9.5 %all-to-all-start.2 = ((bf16[32,2,8192]{2,1,0:T(2,128)(2,1)}), bf16[32,2,8192]{2,1,0:T(2,128)(2,1)}, u32[]{:S(2)}, u32[]{:S(2)}) async-start(bf16[32,2,8192]{2,1,0:T(2,128)(2,1)} %reshape.189), calls=%async_computation.2 | async-start | bytes 2097152 | tf_op jit(solution)/shard_map/all_to_all | solution.py:115
  182.0 3.5 reshape.186
  188.5 5.8 reshape.188
  197.4 8.7 all-to-all-done.2
  206.1 5.8 reshape.190
  215.0 115.3 %while.16 = (s32[]{:T(128)}, f32[4096,128]{1,0:T(8,128)}, f32[]{:T(128)}, bf16[4096,128]{1,0:T(8,128)(2,1)}, bf16[4096,128]{1,0:T(8,128)(2,1)}, /*index=5*/bf16[...) while((s32[]{:T(128)}, f32[4096,128]{1,0:T(8,128)}, ...), condition=%wide.region_4.0_spmd.clone, body=%wide.region_0.4_spmd.clone.sunk | while | flops 1630862848 | bytes 65689848 | solution.py:66
  223.2 4.9 convolution_add_fusion.3
  237.0 5.6 convolution_add_fusion.3
  243.3 3.0 fusion.52
  251.5 5.6 convolution_add_fusion.3
  266.0 5.6 convolution_add_fusion.3
  280.6 5.6 convolution_add_fusion.3
  295.0 5.6 convolution_add_fusion.3
  309.6 5.6 convolution_add_fusion.3
  324.1 5.6 convolution_add_fusion.3
  332.0 17.2 %copy.70 = bf16[1,4096,128]{2,0,1:T(2,128)(2,1)} copy(bf16[1,4096,128]{2,1,0:T(8,128)(2,1)S(1)} %convert_bitcast_fusion) | data formatting | bytes 2097152 | tf_op jit(solution)/shard_map/broadcast_in_dim | solution.py:125
  349.2 23.5 %reduce.4 = bf16[4096,128]{1,0:T(8,128)(2,1)S(1)} reduce(bf16[4096,1,128]{2,1,0:T(2,128)(2,1)} %bitcast.95, bf16[]{:T(256)} %broadcast.113), dimensions={1}, to_apply=%bitcast.75.reduce_sub_computation | reduce | bytes 2097154
  373.8 31.2 %all_to_all.54 = bf16[32,2,8192]{2,1,0:T(2,128)(2,1)S(1)} all-to-all(bf16[32,2,8192]{2,1,0:T(2,128)(2,1)} %reshape.191), channel_id=1, replica_groups=mesh['dp'=8,'ctx'=32] {'ctx'}, dimensions={0} | all-to-all | bytes 2097152 | tf_op jit(solution)/shard_map/all_to_all | solution.py:126
  405.1 3.5 reshape.192
  418.0 79.5 %all-reduce = (f32[]{:T(128)}, f32[]{:T(128)}) all-reduce(f32[]{:T(128)} %get-tuple-element.144, f32[]{:T(128)} %fusion.25), channel_id=1, replica_groups=mesh['dp'=8,'ctx'=32] {'dp','ctx'}, use_global_device_ids=true, to_apply=%region_10.11 | all-reduce | flops 2 | bytes 16 | tf_op jit(solution)/shard_map/psum | solution.py:145
  499.5 120.6 %reduce-scatter.5.cloned.1.call-done = f32[64,16]{0,1:T(8,128)} async-done(((f32[64,512]{0,1:T(8,128)}), f32[64,16]{0,1:T(8,128)}) %reduce-scatter.5.cloned.1.call-update) | async-done | bytes 4112 | tf_op jit(solution)/shard_map/reduce_scatter | solution.py:142
  620.1 18.1 %psum.30 = f32[64,16]{0,1:T(8,128)S(1)} all-reduce(f32[64,16]{0,1:T(8,128)} %reduce-scatter.5.cloned.1.call-done), channel_id=1, replica_groups=mesh['dp'=8,'ctx'=32] {'dp'}, use_global_device_ids=true, to_apply=%region_12.13 | all-reduce | flops 1024 | bytes 8192 | tf_op jit(solution)/shard_map/psum | solution.py:144
  638.2 200.4 %reduce-scatter.3.cloned.1.call-done = f32[256,64]{0,1:T(8,128)} async-done(((f32[8192,64]{0,1:T(8,128)}), f32[256,64]{0,1:T(8,128)}) %reduce-scatter.3.cloned.1.call-update) | async-done | bytes 65552 | tf_op jit(solution)/shard_map/reduce_scatter | solution.py:141
  839.3 67.1 %all-reduce.3.cloned.1.call-done = f32[256,64]{0,1:T(8,128)} async-done(((f32[256,64]{0,1:T(8,128)}), f32[256,64]{0,1:T(8,128)}) %all-reduce.3.cloned.1.call-update) | async-done | bytes 65552 | tf_op jit(solution)/shard_map/psum | solution.py:144
  (136 shorter events, 103.3 us)
Async XLA Ops:
  7.2 114.7 %copy-start = (bf16[1,128,8192]{2,1,0:T(8,128)(2,1)S(1)}, bf16[1,128,8192]{2,1,0:T(8,128)(2,1)}, u32[]{:S(2)}) copy-start(bf16[1,128,8192]{2,1,0:T(8,128)(2,1)} %param.11) | copy-start | bytes 6291460
  55.0 57.2 %all-to-all-start = ((bf16[32,2,8192]{2,1,0:T(2,128)(2,1)}), bf16[32,2,8192]{2,1,0:T(2,128)(2,1)S(1)}, u32[]{:S(2)}, u32[]{:S(2)}) async-start(bf16[32,2,8192]{2,1,0:T(2,128)(2,1)} %reshape.185), calls=%async_computation | async-start | bytes 2097152 | tf_op jit(solution)/shard_map/all_to_all | solution.py:113
  112.2 59.2 %all-to-all-start.1 = ((bf16[32,2,8192]{2,1,0:T(2,128)(2,1)}), bf16[32,2,8192]{2,1,0:T(2,128)(2,1)}, u32[]{:S(2)}, u32[]{:S(2)}) async-start(bf16[32,2,8192]{2,1,0:T(2,128)(2,1)} %reshape.187), calls=%async_computation.1 | async-start | bytes 2097152 | tf_op jit(solution)/shard_map/all_to_all | solution.py:114
  121.9 2.1 copy-start.4
  171.4 34.7 %all-to-all-start.2 = ((bf16[32,2,8192]{2,1,0:T(2,128)(2,1)}), bf16[32,2,8192]{2,1,0:T(2,128)(2,1)}, u32[]{:S(2)}, u32[]{:S(2)}) async-start(bf16[32,2,8192]{2,1,0:T(2,128)(2,1)} %reshape.189), calls=%async_computation.2 | async-start | bytes 2097152 | tf_op jit(solution)/shard_map/all_to_all | solution.py:115
  180.9 439.2 %reduce-scatter.5.cloned.1.call-start = ((), (), s32[]{:S(2)}) async-start(), calls=%async_computation.8 | async-start | bytes 270336 | tf_op jit(solution)/shard_map/reduce_scatter | solution.py:142
  219.3 2.1 copy-start.3
  221.3 1.9 copy-start.1
  233.1 2.1 copy-start.3
  235.1 1.9 copy-start.1
  247.6 2.1 copy-start.3
  249.6 1.9 copy-start.1
  262.1 2.1 copy-start.3
  264.1 1.9 copy-start.1
  276.6 2.1 copy-start.3
  278.6 1.9 copy-start.1
  291.1 2.1 copy-start.3
  293.1 1.9 copy-start.1
  305.6 2.1 copy-start.3
  307.6 1.9 copy-start.1
  320.1 2.1 copy-start.3
  322.1 1.9 copy-start.1
  408.5 3.0 copy-start.5
  411.5 427.1 %reduce-scatter.3.cloned.1.call-start = ((), (), s32[]{:S(2)}) async-start(), calls=%async_computation.6 | async-start | bytes 2162688 | tf_op jit(solution)/shard_map/reduce_scatter | solution.py:141
  413.5 0.8 copy-start.6
  413.5 1.5 copy-start.2
  413.5 492.9 %all-reduce.3.cloned.1.call-start = ((), (), s32[]{:S(2)}) async-start(), calls=%async_computation.7 | async-start | bytes 131072 | tf_op jit(solution)/shard_map/psum | solution.py:144
Sparse Core Ops, SparseCore 0:
  411.6 208.4 reduce-scatter.4
  624.4 214.1 reduce-scatter.2
  840.9 65.3 all-reduce.2
where the time goes:
time: 926 us; the launch traced here: 916 us
  waiting for transfers between devices  397 us (43%)
  other arithmetic  131 us (14%)
  blocking collectives  129 us (14%)
  local copies, waits for them, and re-layouts  111 us (12%)
  matrix products  91.1 us (10%)
  starting transfers between devices  31.9 us (3%)
  between operations  20.1 us (2%)
    reduce_scatter x1, waiting for transfers between devices, body(): lax.psum_scatter(down_part, 'ctx', scatter_dimension=0, tiled=True)  200 us
    reduce_scatter x1, waiting for transfers between devices, body(): lax.psum_scatter(up_part, 'ctx', scatter_dimension=1, tiled=True)  121 us
    unnamed x5, other arithmetic  95.8 us
    psum x1, blocking collectives, body(): curv_total = lax.psum(curv_piece, ('dp', 'ctx'))  79.5 us
    psum x1, waiting for transfers between devices, body(): down_own, up_own = lax.psum((down_rows, up_cols_sum), 'dp')  67.1 us
    dot_general x8, matrix products, block_step(): jnp.einsum('qk,qd->kd', probs_bf, cotangent, preferred_element_type=jnp.f...  44 us
    broadcast_in_dim x4, local copies, waits for them, and re-layouts, copy_heads(): jnp.repeat(per_kv.reshape(1, seq_len, kv_heads, HEAD_WIDTH), GROUP, axis=2)  34.6 us
    unnamed x23, local copies, waits for them, and re-layouts  33.3 us
  transfers between devices with their start and end apart: 6, of which 4 were waited for; matrix products, arithmetic and copies ran while one was open for 13% of the time, Pallas kernels for 0%

commit v1 on v0

v1 whole, which is shorter than its diff:
```python
import functools
import math

import jax
import jax.numpy as jnp
from jax import lax
from jax.experimental import pallas as pl
from jax.experimental.pallas import tpu as pltpu
from jax.sharding import PartitionSpec as P

HW = 128
GROUP = 8
RANK = 64
NZ, NY, NX = 8, 4, 4
ROWS = 256
CHUNK = 2048
F32 = jnp.float32
BF = jnp.bfloat16
MESH = pl.DeviceIdType.MESH
NN = (((1,), (0,)), ((), ()))
NT = (((1,), (1,)), ((), ()))
VM = pl.BlockSpec(memory_space=pltpu.VMEM)
SM = pl.BlockSpec(memory_space=pltpu.SMEM)


def dot(a, b, dims=NN):
    return lax.dot_general(a, b, dims, preferred_element_type=F32)


def place():
    ctx = lax.axis_index("ctx")
    return ctx // NY, lax.rem(ctx, NY)


class Flow:
    def __init__(self, index, size, here, block, peer, send_sem, recv_sem):
        self.index, self.size, self.here = index, size, here
        self.block, self.peer = block, peer
        self.send_sem, self.recv_sem = send_sem, recv_sem
        self.step, self.sent = 0, []

    def copy(self, step, way, origin):
        half = None if step < self.size // 2 else way
        ref = self.block(lax.rem(origin + 2 * self.size, self.size), half)
        to = lax.rem(self.here + (1 if way == 0 else self.size - 1), self.size)
        return pltpu.make_async_remote_copy(
            src_ref=ref,
            dst_ref=ref,
            send_sem=self.send_sem.at[self.index, step - 1, way],
            recv_sem=self.recv_sem.at[self.index, step - 1, way],
            device_id=self.peer(to),
            device_id_type=MESH,
        )

    def send(self):
        self.step += 1
        for way, sign in ((0, -1), (1, 1)):
            copy = self.copy(self.step, way, self.here + sign * (self.step - 1))
            copy.start()
            self.sent.append(copy)

    def receive(self):
        for way, sign in ((0, -1), (1, 1)):
            self.copy(self.step, way, self.here + sign * self.step).wait_recv()

    def last(self):
        return self.step == self.size // 2


def gather_kernel(hidden, queries, keys, down, direction, cosine, sine, gath, qT, send_sem, recv_sem):
    z, y = place()
    barrier = pltpu.get_barrier_semaphore()

    def at(zz, yy):
        return {"ctx": zz * NY + yy}

    def ring(value, size):
        return lax.rem(value + size, size)

    for target in (
        at(z, ring(y + 1, NY)),
        at(z, ring(y - 1, NY)),
        at(ring(z + 1, NZ), y),
        at(ring(z - 1, NZ), y),
    ):
        pl.semaphore_signal(barrier, inc=1, device_id=target, device_id_type=MESH)

    cos, sin = cosine[...], sine[...]

    def turn(u):
        u = u.astype(F32)
        return u * cos + pltpu.roll(u, HW // 2, 1) * sin

    for g in range(4):
        gath[g, z, y] = turn(keys[:, g * HW : (g + 1) * HW]).astype(BF)
    gath[4, z, y, 0:RANK, :] = dot(down[...], hidden[...], NT).astype(BF)
    gath[4, z, y, RANK:HW, :] = dot(direction[...], hidden[...], NT).astype(BF)
    pl.semaphore_wait(barrier, 4)

    parts = (slice(3, 5), slice(0, 3))

    def cut(ref, half):
        if half is None:
            return ref
        return ref.at[:, half * 64 : half * 64 + 64, :]

    count = [0]

    def make_y(part, zz):
        count[0] += 1
        return Flow(
            count[0] - 1, NY, y,
            lambda origin, half: cut(gath.at[part, zz, origin], half),
            lambda to: at(z, to), send_sem, recv_sem,
        )

    def make_z(part, yy):
        count[0] += 1
        return Flow(
            count[0] - 1, NZ, z,
            lambda origin, half: cut(gath.at[part, origin, yy], half),
            lambda to: at(to, y), send_sem, recv_sem,
        )

    first_y = make_y(parts[0], z)
    first_z = make_z(parts[1], y)
    flows, done = [first_y, first_z], []
    flows.append(make_z(parts[0], y))
    flows.append(make_y(parts[1], z))
    for flow in flows:
        flow.send()

    scale = math.log2(math.e) / math.sqrt(HW)

    def rotate_queries(i, _):
        for h in range(ROWS // HW):
            u = queries[:, pl.ds(pl.multiple_of(i * ROWS + h * HW, HW), HW)]
            qT[i, :, h * HW : (h + 1) * HW] = jnp.transpose(turn(u) * scale).astype(BF)
        return 0

    lax.fori_loop(0, qT.shape[0], rotate_queries, 0)

    while flows:
        fresh = []
        for flow in list(flows):
            flow.receive()
            step = flow.step
            if flow.last():
                flows.remove(flow)
                done.append(flow)
            else:
                flow.send()
            near = (step,) if step == flow.size // 2 else (-step, step)
            if flow is first_y:
                fresh += [make_z(parts[0], ring(y + o, NY)) for o in near]
            if flow is first_z:
                fresh += [make_y(parts[1], ring(z + o, NZ)) for o in near]
        for flow in fresh:
            flow.send()
        flows += fresh
    for flow in done:
        for copy in flow.sent:
            copy.wait_send()


def gather(hidden, queries, keys, down, direction, cosine, sine):
    return pl.pallas_call(
        gather_kernel,
        out_shape=(
            jax.ShapeDtypeStruct((5, NZ, NY, HW, HW), BF),
            jax.ShapeDtypeStruct((queries.shape[1] // ROWS, HW, ROWS), BF),
        ),
        in_specs=[VM] * 7,
        out_specs=(VM, VM),
        scratch_shapes=[
            pltpu.SemaphoreType.DMA((14, 4, 2)),
            pltpu.SemaphoreType.DMA((14, 4, 2)),
        ],
        compiler_params=pltpu.CompilerParams(
            collective_id=0, has_side_effects=True, vmem_limit_bytes=48 * 1024 * 1024
        ),
    )(hidden, queries, keys, down, direction, cosine, sine)


def attend_kernel(
    info, gath, qT, wT, up, mixed_ref, upT_ref, curv_ref, s_buf, p_buf, vT, grad, oacc, w_buf, curv_acc
):
    kvh = 4
    blocks = NZ * NY
    span = blocks * HW
    per = CHUNK // HW
    me, live = info[0], info[1]
    chunks = lax.div(me, per) + 1
    per_g = GROUP * HW // ROWS
    total = kvh * per_g

    def tangents(j, _):
        for b in range(per):
            vv = dot(wT[...], gath[4, j * per + b]).astype(BF)
            for g in range(kvh):
                vT[g, 0:HW, pl.ds(pl.multiple_of(j * CHUNK + b * HW, HW), HW)] = vv[g * HW : (g + 1) * HW]
        return 0

    lax.fori_loop(0, chunks, tangents, 0)
    ones = jnp.where(lax.broadcasted_iota(jnp.int32, (16, span), 0) == 0, 1.0, 0.0).astype(BF)
    for g in range(kvh):
        vT[g, HW : HW + 16, :] = ones
    grad[...] = jnp.zeros_like(grad)
    curv_acc[...] = jnp.zeros_like(curv_acc)
    qpos = me * HW + lax.rem(lax.broadcasted_iota(jnp.int32, (1, ROWS), 1), HW)
    liverow = (qpos < live).astype(F32)

    def step(i, score, weigh, back, m_prev):
        even, odd = lax.rem(i, 2), lax.rem(i + 1, 2)
        if weigh:
            oacc[...] = jnp.zeros_like(oacc)
        q = qT[i] if score else None

        def body(j, mx):
            ks = pl.multiple_of(j * CHUNK, CHUNK)
            if back:
                grad[lax.div(i - 2, per_g), :, pl.ds(ks, CHUNK)] += dot(
                    w_buf[even], p_buf[even, pl.ds(ks, CHUNK), :], NT
                )
            if weigh:
                p = jnp.exp2(s_buf[odd, pl.ds(ks, CHUNK), :] - m_prev).astype(BF)
                p_buf[odd, pl.ds(ks, CHUNK), :] = p
                oacc[...] += dot(vT[lax.div(i - 1, per_g), :, pl.ds(ks, CHUNK)], p)
            if score:
                kc = gath[lax.div(i, per_g), pl.ds(j * per, per)].reshape(CHUNK, HW)
                s = dot(kc, q)
                kpos = ks + lax.broadcasted_iota(jnp.int32, (CHUNK, ROWS), 0)
                s = jnp.where(kpos <= qpos, s, -1e30)
                s_buf[even, pl.ds(ks, CHUNK), :] = s
                mx = jnp.maximum(mx, jnp.max(s.reshape(CHUNK // 8, 8, ROWS), axis=0))
            return mx

        mx = lax.fori_loop(0, chunks, body, jnp.full((8, ROWS), -1e30, F32))
        if weigh:
            o = oacc[...]
            inv = 1.0 / o[HW : HW + 1]
            out = o[0:HW] * inv * liverow
            curv_acc[...] += jnp.sum((out * out).reshape(HW // 8, 8, ROWS), axis=0)
            w_buf[odd] = (out * inv).astype(BF)
        return jnp.max(mx, axis=0, keepdims=True)

    top = step(0, True, False, False, None)
    top = step(1, True, True, False, top)
    top = lax.fori_loop(2, total, lambda i, m: step(i, True, True, True, m), top)
    step(total, False, True, True, top)
    step(total + 1, False, False, True, None)

    mixed_ref[...] = jnp.zeros_like(mixed_ref)
    upT_ref[...] = jnp.zeros_like(upT_ref)

    def finish(j, _):
        ks = pl.multiple_of(j * CHUNK, CHUNK)
        grads = [grad[g, :, pl.ds(ks, CHUNK)].astype(BF) for g in range(kvh)]
        mixed = sum(dot(up[:, g * HW : (g + 1) * HW], grads[g]) for g in range(kvh)).astype(BF)
        for b in range(per):
            cols = slice(b * HW, (b + 1) * HW)
            mixed_ref[j * per + b] = mixed[:, cols]
            act = gath[4, j * per + b, 0:RANK, :]
            for g in range(kvh):
                upT_ref[g * HW : (g + 1) * HW, :] += dot(grads[g][:, cols], act, NT)
        return 0

    lax.fori_loop(0, chunks, finish, 0)
    both = curv_acc[:, 0:HW] + curv_acc[:, HW : 2 * HW]
    row = lax.broadcasted_iota(jnp.int32, (8, HW), 0)
    lane = lax.broadcasted_iota(jnp.int32, (8, HW), 1)
    mine = ((me * HW + lane) < live).astype(F32)
    curv_ref[...] = jnp.where(
        row == 0, jnp.sum(both, axis=0, keepdims=True), jnp.where(row == 1, mine, 0.0)
    )


def attention(info, gath, qT, wT, up):
    span = NZ * NY * HW
    return pl.pallas_call(
        attend_kernel,
        out_shape=(
            jax.ShapeDtypeStruct((NZ * NY, RANK, HW), BF),
            jax.ShapeDtypeStruct((4 * HW, RANK), F32),
            jax.ShapeDtypeStruct((8, HW), F32),
        ),
        in_specs=[SM, VM, VM, VM, VM],
        out_specs=(VM, VM, VM),
        scratch_shapes=[
            pltpu.VMEM((2, span, ROWS), F32),
            pltpu.VMEM((2, span, ROWS), BF),
            pltpu.VMEM((4, HW + 16, span), BF),
            pltpu.VMEM((4, HW, span), F32),
            pltpu.VMEM((HW + 16, ROWS), F32),
            pltpu.VMEM((2, HW, ROWS), BF),
            pltpu.VMEM((8, ROWS), F32),
        ],
        compiler_params=pltpu.CompilerParams(vmem_limit_bytes=56 * 1024 * 1024),
    )(info, gath, qT, wT, up)


def reduce_kernel(
    mixed, upT, curv, hidden, direction, up_direction, down_out, up_out, curv_out,
    got_y, sum_y, got_z, part, got_core, sum_core, got_x, sum_x, ups, got_dy, got_uy, sum_dy, got_dz, all_dp,
    send_sem, recv_sem,
):
    z, y = place()
    ctx = lax.axis_index("ctx")
    dp = lax.axis_index("dp")
    x, core = dp // 2, lax.rem(dp, 2)
    barrier = pltpu.get_barrier_semaphore()

    def at_y(o):
        return {"ctx": z * NY + lax.rem(y + o, NY)}

    def at_z(o):
        return {"ctx": lax.rem(z + o, NZ) * NY + y}

    def at_dp(o):
        return {"dp": lax.rem(dp + o, 8)}

    for o in range(1, NY):
        pl.semaphore_signal(barrier, inc=1, device_id=at_y(o), device_id_type=MESH)
    for o in range(1, NZ):
        pl.semaphore_signal(barrier, inc=1, device_id=at_z(o), device_id_type=MESH)
    for o in range(1, 8):
        pl.semaphore_signal(barrier, inc=1, device_id=at_dp(o), device_id_type=MESH)

    used = [0]
    sent = []

    def send(src, dst, to):
        copy = pltpu.make_async_remote_copy(
            src_ref=src, dst_ref=dst, send_sem=send_sem.at[used[0]], recv_sem=recv_sem.at[used[0]],
            device_id=to, device_id_type=MESH,
        )
        used[0] += 1
        copy.start()
        sent.append(copy)
        return copy

    pl.semaphore_wait(barrier, 17)

    copies = [
        send(mixed.at[:, lax.rem(y + o, NY)], got_y.at[o - 1], at_y(o)) for o in range(1, NY)
    ]
    for i in range(32):
        block = upT[16 * i : 16 * i + 16, :]
        ups[i % NY, i // NY] = jnp.concatenate([block[0:8], block[8:16]], axis=1)
    for i in range(NY):
        ups[i, NZ] = curv[...]

    def squares(i, acc):
        d = direction[:, pl.ds(pl.multiple_of(i * 512, 512), 512)].astype(F32)
        return acc + jnp.sum((d * d).reshape(8, 8, 512), axis=0)

    squared = jnp.sum(lax.fori_loop(0, 16, squares, jnp.zeros((8, 512), F32)))
    ud = up_direction[...].astype(F32)
    squared = squared + jnp.sum(ud * ud)

    for copy in copies:
        copy.wait_recv()

    def add_y(i, _):
        acc = mixed[i, y].astype(F32)
        for o in range(NY - 1):
            acc = acc + got_y[o, i].astype(F32)
        sum_y[i] = acc.astype(BF)
        return 0

    lax.fori_loop(0, NZ, add_y, 0)
    copies = [
        send(sum_y.at[lax.rem(z + o, NZ)], got_z.at[o - 1], at_z(o)) for o in range(1, NZ)
    ]
    for copy in copies:
        copy.wait_recv()
    own = sum_y[z].astype(F32)
    for o in range(NZ - 1):
        own = own + got_z[o].astype(F32)
    own = own.astype(BF)

    def down(i, _):
        d = dot(own, hidden[:, pl.ds(pl.multiple_of(i * 256, 256), 256)])
        for r in range(8):
            rows = d[8 * r : 8 * r + 8]
            part[r // 2, r % 2, i] = jnp.concatenate([rows[:, 0:HW], rows[:, HW:]], axis=0).astype(BF)
        return 0

    lax.fori_loop(0, 32, down, 0)

    copy = send(part.at[:, 1 - core], got_core, {"dp": x * 2 + 1 - core})
    copy.wait_recv()

    def add_core(i, _):
        for xx in range(NX):
            sum_core[xx, i] = (part[xx, core, i].astype(F32) + got_core[xx, i].astype(F32)).astype(BF)
        return 0

    lax.fori_loop(0, 32, add_core, 0)
    copies = [
        send(sum_core.at[lax.rem(x + o, NX)], got_x.at[o - 1], {"dp": lax.rem(x + o, NX) * 2 + core})
        for o in range(1, NX)
    ]
    for copy in copies:
        copy.wait_recv()

    def add_x(i, _):
        for yy in range(NY):
            acc = sum_core[x, i * NY + yy].astype(F32)
            for o in range(NX - 1):
                acc = acc + got_x[o, i * NY + yy].astype(F32)
            sum_x[yy, i] = acc.astype(BF)
        return 0

    lax.fori_loop(0, NZ, add_x, 0)
    copies = []
    for o in range(1, NY):
        to = lax.rem(y + o, NY)
        copies.append(send(sum_x.at[to], got_dy.at[o - 1], at_y(o)))
        copies.append(send(ups.at[to], got_uy.at[o - 1], at_y(o)))
    for copy in copies:
        copy.wait_recv()
    scal = ups[y, NZ]
    for o in range(NY - 1):
        scal = scal + got_uy[o, NZ]
    for i in range(NZ):
        acc = sum_x[y, i].astype(F32)
        upa = ups[y, i]
        for o in range(NY - 1):
            acc = acc + got_dy[o, i].astype(F32)
            upa = upa + got_uy[o, i]
        sum_dy[i, 0:16] = acc
        sum_dy[i, 16:24] = upa
        sum_dy[i, 24:32] = scal
    copies = [
        send(sum_dy.at[lax.rem(z + o, NZ)], got_dz.at[o - 1], at_z(o)) for o in range(1, NZ)
    ]
    for copy in copies:
        copy.wait_recv()
    acc = sum_dy[z]
    for o in range(NZ - 1):
        acc = acc + got_dz[o]
    all_dp[dp] = acc
    copies = [send(all_dp.at[dp], all_dp.at[dp], at_dp(o)) for o in range(1, 8)]
    for o in range(1, 8):
        slot = lax.rem(dp + 8 - o, 8)
        base = used[0] - 7 + o - 1
        pltpu.make_async_remote_copy(
            src_ref=all_dp.at[slot], dst_ref=all_dp.at[slot], send_sem=send_sem.at[base],
            recv_sem=recv_sem.at[base], device_id=at_dp(o), device_id_type=MESH,
        ).wait_recv()
    tail = all_dp[0, 16:32]
    for r in range(1, 8):
        tail = tail + all_dp[r, 16:32]
    curv_sum = jnp.sum(tail[8:9])
    count = jnp.sum(tail[9:10])
    rescale = squared / (curv_sum + 1e-06)
    for r in range(8):
        down_out[8 * r : 8 * r + 8, 0:HW] = all_dp[r, 0:8] * rescale
        down_out[8 * r : 8 * r + 8, HW : 2 * HW] = all_dp[r, 8:16] * rescale
    up_out[0:8, :] = tail[0:8, 0:RANK] * rescale
    up_out[8:16, :] = tail[0:8, RANK:HW] * rescale
    curv_out[...] = jnp.full((8, HW), curv_sum / count, F32)
    for copy in sent:
        copy.wait_send()


def reduce(mixed, upT, curv, hidden, direction, up_direction):
    return pl.pallas_call(
        reduce_kernel,
        out_shape=(
            jax.ShapeDtypeStruct((RANK, 256), F32),
            jax.ShapeDtypeStruct((16, RANK), F32),
            jax.ShapeDtypeStruct((8, HW), F32),
        ),
        in_specs=[VM] * 6,
        out_specs=(VM, VM, VM),
        scratch_shapes=[
            pltpu.VMEM((NY - 1, NZ, RANK, HW), BF),
            pltpu.VMEM((NZ, RANK, HW), BF),
            pltpu.VMEM((NZ - 1, RANK, HW), BF),
            pltpu.VMEM((NX, 2, 32, 16, HW), BF),
            pltpu.VMEM((NX, 32, 16, HW), BF),
            pltpu.VMEM((NX, 32, 16, HW), BF),
            pltpu.VMEM((NX - 1, 32, 16, HW), BF),
            pltpu.VMEM((NY, NZ, 16, HW), BF),
            pltpu.VMEM((NY, NZ + 1, 8, HW), F32),
            pltpu.VMEM((NY - 1, NZ, 16, HW), BF),
            pltpu.VMEM((NY - 1, NZ + 1, 8, HW), F32),
            pltpu.VMEM((NZ, 32, HW), F32),
            pltpu.VMEM((NZ - 1, 32, HW), F32),
            pltpu.VMEM((8, 32, HW), F32),
            pltpu.SemaphoreType.DMA((40,)),
            pltpu.SemaphoreType.DMA((40,)),
        ],
        compiler_params=pltpu.CompilerParams(
            collective_id=1, has_side_effects=True, vmem_limit_bytes=48 * 1024 * 1024
        ),
    )(mixed, upT, curv, hidden, direction, up_direction)


def body(hidden, queries, keys, down, up, direction, up_direction, window, lengths):
    seq = hidden.shape[1]
    span = seq * NZ * NY
    ctx = lax.axis_index("ctx")
    position = window[0] * span + ctx * seq + jnp.arange(seq, dtype=jnp.int32)
    inv_freq = jnp.exp(jnp.arange(HW // 2, dtype=F32) * (-2.0 * math.log(1000000.0) / HW))
    angles = position.astype(F32)[:, None] * inv_freq
    cosine, sine = jnp.cos(angles), jnp.sin(angles)
    cosine = jnp.concatenate([cosine, cosine], axis=1)
    sine = jnp.concatenate([-sine, sine], axis=1)
    info = jnp.stack([ctx.astype(jnp.int32), lengths[0] - window[0] * span])
    wT = jnp.concatenate([up_direction, up], axis=0).T
    gath, qT = gather(hidden[0], queries[0], keys[0], down.T, direction.T, cosine, sine)
    mixed, upT, curv = attention(info, gath.reshape(5, NZ * NY, HW, HW), qT, wT, up)
    down_out, up_out, curv_out = reduce(
        mixed.reshape(NZ, NY, RANK, HW), upT, curv, hidden[0], direction.T, up_direction
    )
    return down_out.T, up_out.T, curv_out[0, 0]


def solution(mesh):
    placed = (
        P("dp", "ctx", None),
        P("dp", "ctx", None),
        P("dp", "ctx", None),
        P(),
        P(),
        P(),
        P(),
        P("dp"),
        P("dp"),
    )
    return jax.shard_map(
        body,
        mesh=mesh,
        in_specs=placed,
        out_specs=(P("ctx", None), P(None, "ctx"), P()),
        check_vma=False,
    )
```

time: 926 us -> 158 us (0.17); the launches traced: 916 us -> 158 us
  waiting for transfers between devices: 397 us -> 0 us
  Pallas kernels: 0 us -> 142 us
  other arithmetic: 131 us -> 1.84 us
  blocking collectives: 129 us -> 0 us
  local copies, waits for them, and re-layouts: 111 us -> 11.9 us
  matrix products: 91.1 us -> 0 us
  starting transfers between devices: 31.9 us -> 0 us
  between operations: 20.1 us -> 2.02 us
    reduce_scatter x2 -> x0, waiting for transfers between devices: 321 us -> none  [the longest x1 200 us: body(): lax.psum_scatter(down_part, 'ctx', scatter_dimension=0, tiled=True)]
    pallas_call x0 -> x3, Pallas kernels: none -> 142 us  [the longest x1 69.9 us: reduce(): pl.pallas_call(reduce_kernel, out_shape=(jax.ShapeDtypeStruct((RANK, 256)...]
    psum x2 -> x0, blocking collectives: 97.6 us -> none  [the longest x1 79.5 us: body(): curv_total = lax.psum(curv_piece, ('dp', 'ctx'))]
    unnamed x5 -> x0, other arithmetic: 95.8 us -> none
    dot_general x29 -> x0, matrix products: 91.1 us -> none  [the longest x8 44 us: block_step(): jnp.einsum('qk,qd->kd', probs_bf, cotangent, preferred_element_type=jnp.f...]
    psum x1 -> x0, waiting for transfers between devices: 67.1 us -> none  [body(): down_own, up_own = lax.psum((down_rows, up_cols_sum), 'dp')]
    broadcast_in_dim x5 -> x0, local copies, waits for them, and re-layouts: 51.8 us -> none  [the longest x4 34.6 us: copy_heads(): jnp.repeat(per_kv.reshape(1, seq_len, kv_heads, HEAD_WIDTH), GROUP, axis=2)]
    all_to_all x3 -> x0, starting transfers between devices: 31.3 us -> none  [the longest x1 12.2 us: body(): lax.all_to_all(rot_query, 'ctx', split_axis=2, concat_axis=1, tiled=True)]
  transfers between devices with their start and end apart: 6 -> 0, of which waited for: 4 -> 0; matrix products, arithmetic and copies ran while one was open for 13% -> 0% of each run, Pallas kernels for 0% -> 0%
where the time goes in v1:
time: 158 us
  Pallas kernels  142 us (90%)
  local copies, waits for them, and re-layouts  11.9 us (8%)
  between operations  2.02 us (1%)
  other arithmetic  1.84 us (1%)
    pallas_call x1, Pallas kernels, reduce(): pl.pallas_call(reduce_kernel, out_shape=(jax.ShapeDtypeStruct((RANK, 256)...  69.9 us
    pallas_call x1, Pallas kernels, gather(): pl.pallas_call(gather_kernel, out_shape=(jax.ShapeDtypeStruct((5, NZ, NY,...  48.1 us
    pallas_call x1, Pallas kernels, attention(): pl.pallas_call(attend_kernel, out_shape=(jax.ShapeDtypeStruct((NZ * NY, R...  23.8 us
    unnamed x26, local copies, waits for them, and re-layouts  11.4 us

profile of v1, /device:TPU:1, one launch (start us, length us, event | category | flops | bytes accessed | tf_op | source)
XLA Modules:
  0.0 157.5 jit_solution(104074435884861005)
XLA Ops:
  1.9 0.7 pad_add_fusion.info
  2.6 1.0 copy.13
  3.6 1.0 copy.12
  4.5 0.8 maximum_bitcast_fusion.wT
  5.3 0.3 fusion
  5.6 0.1 pad_maximum_fusion
  5.7 0.0 copy-start.1
  5.7 1.2 copy-done.1
  6.9 0.0 copy-start.4
  6.9 1.2 copy-done.4
  8.2 0.0 copy-start.5
  8.2 1.2 copy-done.5
  9.4 0.0 copy-start.9
  9.4 0.9 copy-done.9
  10.3 0.0 copy-start
  10.3 0.0 copy-start.2
  10.3 0.0 copy-start.7
  10.3 48.1 %shard_map.112 = (bf16[5,8,4,128,128]{4,3,2,1,0:T(8,128)(2,1)}, bf16[16,128,256]{2,1,0:T(8,128)(2,1)S(1)}) custom-call(bf16[128,8192]{1,0:T(8,128)(2,1)} %bitcast.17, bf16[128,4096]{1,0:T(8,128)(2,1)S(1)} %bitcast.21, bf16[128,512]{1,0:T(8,128)(2,1)S(1)} %bitcast.24, bf16[64,8192]{1,0:T(8,128)(2,1)S(1)} %bitcast.22, bf16[64,8192]{1,0:T(8,128)(2,1)S(1)} %bitcast.19, ...), custom_call_target="tpu_custom_call" | custom-call | tf_op jit(solution)/shard_map/pallas_call | solution.py:167
  58.4 0.0 copy-start.3
  58.4 1.0 copy-done.3
  59.4 23.8 %shard_map.113 = (bf16[32,64,128]{2,1,0:T(8,128)(2,1)}, f32[512,64]{1,0:T(8,128)}, f32[8,128]{1,0:T(8,128)}) custom-call(s32[2]{0:T(128)} %pad_add_fusion.info, bf16[5,32,128,128]{3,2,1,0:T(8,128)(2,1)} %bitcast.27, bf16[16,128,256]{2,1,0:T(8,128)(2,1)} %copy-done.3, bf16[512,128]{1,0:T(8,128)(2,1)} %maximum_bitcast_fusion.wT, bf16[64,512]{1,0:T(8,128)(2,1)} %up.1), custom_call_target="tpu_custom_call" | custom-call | tf_op jit(solution)/shard_map/pallas_call | solution.py:280
  83.2 0.0 copy-done
  83.2 0.0 copy-done.2
  83.2 0.0 copy-done.7
  83.2 0.0 copy-start.6
  83.2 1.0 copy-done.6
  84.2 0.9 copy-done.8
  85.2 0.7 copy-done.10
  85.8 69.9 %shard_map.114 = (f32[64,256]{1,0:T(8,128)S(1)}, f32[16,64]{1,0:T(8,128)S(1)}, f32[8,128]{1,0:T(8,128)S(1)}) custom-call(bf16[8,4,64,128]{3,2,1,0:T(8,128)(2,1)S(1)} %bitcast.23, f32[512,64]{1,0:T(8,128)S(1)} %copy-done.8, f32[8,128]{1,0:T(8,128)S(1)} %copy-done.10, bf16[128,8192]{1,0:T(8,128)(2,1)S(1)} %bitcast.18, bf16[64,8192]{1,0:T(8,128)(2,1)S(1)} %bitcast.20, ...), custom_call_target="tpu_custom_call" | custom-call | tf_op jit(solution)/shard_map/pallas_call | solution.py:469
  155.8 0.5 slice.3
  156.3 0.6 copy.18
  156.9 0.6 copy.19
  (4 shorter events, 0.0 us)
Async XLA Ops:
  5.7 1.2 copy-start.1
  6.9 1.2 copy-start.4
  8.2 1.2 copy-start.5
  9.4 0.9 copy-start.9
  10.3 72.9 %copy-start = (bf16[1,128,8192]{2,1,0:T(8,128)(2,1)S(1)}, bf16[1,128,8192]{2,1,0:T(8,128)(2,1)}, u32[]{:S(2)}) copy-start(bf16[1,128,8192]{2,1,0:T(8,128)(2,1)} %param.9) | copy-start | bytes 6291460
  10.3 72.9 %copy-start.2 = (bf16[8192,64]{0,1:T(8,128)(2,1)S(1)}, bf16[8192,64]{0,1:T(8,128)(2,1)}, u32[]{:S(2)}) copy-start(bf16[8192,64]{0,1:T(8,128)(2,1)} %param.14) | copy-start | bytes 3145732
  10.3 72.9 %copy-start.7 = (bf16[64,512]{1,0:T(8,128)(2,1)S(1)}, bf16[64,512]{1,0:T(8,128)(2,1)}, u32[]{:S(2)}) copy-start(bf16[64,512]{1,0:T(8,128)(2,1)} %up_direction.1) | copy-start | bytes 196612
  58.4 1.0 copy-start.3
  83.2 1.0 copy-start.6
  84.2 0.9 copy-start.8
  85.2 0.7 copy-start.10

commit v2 on v1

v2 whole, which is shorter than its diff:
```python
import functools
import math

import jax
import jax.numpy as jnp
from jax import lax
from jax.experimental import pallas as pl
from jax.experimental.pallas import tpu as pltpu
from jax.sharding import PartitionSpec as P

HW = 128
GROUP = 8
RANK = 64
NZ, NY, NX = 8, 4, 4
ROWS = 256
CHUNK = 2048
SUB = 256
F32 = jnp.float32
BF = jnp.bfloat16
MESH = pl.DeviceIdType.MESH
NN = (((1,), (0,)), ((), ()))
NT = (((1,), (1,)), ((), ()))
VM = pl.BlockSpec(memory_space=pltpu.VMEM)
SM = pl.BlockSpec(memory_space=pltpu.SMEM)


def dot(a, b, dims=NN):
    return lax.dot_general(a, b, dims, preferred_element_type=F32)


def place():
    ctx = lax.axis_index("ctx")
    return ctx // NY, lax.rem(ctx, NY)


class Flow:
    def __init__(self, index, size, here, block, peer, sems):
        self.index, self.size, self.here = index, size, here
        self.block, self.peer = block, peer
        self.send_sem, self.recv_sem = sems
        self.step = 0

    def copy(self, step, way, offset):
        half = None if step < self.size // 2 else way
        ref = self.block(lax.rem(self.here + offset + self.size, self.size), half)
        to = lax.rem(self.here + (1 if way == 0 else self.size - 1), self.size)
        return pltpu.make_async_remote_copy(
            src_ref=ref,
            dst_ref=ref,
            send_sem=self.send_sem.at[self.index, step - 1, way],
            recv_sem=self.recv_sem.at[self.index, step - 1, way],
            device_id=self.peer(to),
            device_id_type=MESH,
        )

    def send(self):
        self.step += 1
        for way, sign in ((0, -1), (1, 1)):
            self.copy(self.step, way, sign * (self.step - 1)).start()

    def receive(self):
        for way, sign in ((0, -1), (1, 1)):
            self.copy(self.step, way, sign * self.step).wait_recv()

    def advance(self):
        self.receive()
        if self.step == self.size // 2:
            return True
        self.send()
        return False

    def drain(self):
        for step in range(1, self.size // 2 + 1):
            for way, sign in ((0, -1), (1, 1)):
                self.copy(step, way, sign * (step - 1)).wait_send()


def cut(ref, half, axis):
    if half is None:
        return ref
    rows = pl.ds(half * 64, 64)
    return ref.at[(slice(None),) * axis + (rows,)]


def attend_kernel(
    info, hidden, queries, keys, down, direction, cosine, sine, wT, up,
    mixed_ref, upT_ref, curv_ref,
    gath, qT, s_even, s_odd, p_even, p_odd, vT, grad, oacc, w_even, w_odd, curv_acc, send_sem, recv_sem,
):
    z, y = place()
    barrier = pltpu.get_barrier_semaphore()

    def at(zz, yy):
        return {"ctx": zz * NY + yy}

    ys = [lax.rem(y + o, NY) for o in range(NY)]
    zs = [lax.rem(z + o, NZ) for o in range(NZ)]
    for target in (at(z, ys[1]), at(z, ys[3]), at(zs[1], y), at(zs[7], y)):
        pl.semaphore_signal(barrier, inc=1, device_id=target, device_id_type=MESH)

    cos, sin = cosine[...], sine[...]

    def turn(u):
        u = u.astype(F32)
        return u * cos + pltpu.roll(u, HW // 2, 1) * sin

    gath[0, z, y, 0:RANK, :] = dot(down[...], hidden[...], NT).astype(BF)
    gath[0, z, y, RANK:HW, :] = dot(direction[...], hidden[...], NT).astype(BF)
    for g in range(4):
        gath[1 + g, z, y] = turn(keys[:, g * HW : (g + 1) * HW]).astype(BF)
    pl.semaphore_wait(barrier, 4)

    made = []
    sems = (send_sem, recv_sem)

    def ring_y(part, zz):
        flow = Flow(len(made), NY, y, lambda o, half: cut(gath.at[part, zz, o], half, 0), lambda to: at(z, to), sems)
        made.append(flow)
        return flow

    def ring_z(part, yy):
        flow = Flow(len(made), NZ, z, lambda o, half: cut(gath.at[part, o, yy], half, 0), lambda to: at(to, y), sems)
        made.append(flow)
        return flow

    def ring_z_all(part):
        flow = Flow(
            len(made), NZ, z, lambda o, half: cut(gath.at[part, o], half, 1), lambda to: at(to, y), sems
        )
        made.append(flow)
        return flow

    def ring_z_pair(part):
        flow = Flow(
            len(made), NZ, z, lambda o, half: cut(gath.at[part, o, y], half, 1), lambda to: at(to, y), sems
        )
        made.append(flow)
        return flow

    def ring_y_all(part):
        flow = Flow(
            len(made), NY, y, lambda o, half: cut(gath.at[part, :, o], half, 2), lambda to: at(z, to), sems
        )
        made.append(flow)
        return flow

    first_y, first_z = ring_y(0, z), ring_z(1, y)
    lanes = [ring_z(0, y), ring_y(1, z)]
    for flow in [first_y, first_z] + lanes:
        flow.send()
    heads = [first_y, first_z]

    scale = math.log2(math.e) / math.sqrt(HW)

    def rotate_queries(i, _):
        for h in range(ROWS // HW):
            u = queries[:, pl.ds(pl.multiple_of(i * ROWS + h * HW, HW), HW)]
            qT[i, :, h * HW : (h + 1) * HW] = jnp.transpose(turn(u) * scale).astype(BF)
        return 0

    lax.fori_loop(0, qT.shape[0], rotate_queries, 0)

    late = {}
    for slot in range(1, 7):
        fresh = []
        for flow in list(heads):
            end = flow.advance()
            step = flow.step if not end else flow.size // 2
            step = step if end else step - 1
            near = (step,) if end else (flow.size - step, step)
            for o in near:
                fresh.append(ring_z(0, ys[o]) if flow is first_y else ring_y(1, zs[o]))
            if end:
                heads.remove(flow)
        for flow in list(lanes):
            if flow.advance():
                lanes.remove(flow)
        for flow in fresh:
            flow.send()
        lanes += fresh
        if slot == 2:
            late["z34"] = ring_z_pair(slice(3, 5))
            late["z34"].send()
        elif slot <= 6 and "z34" in late:
            if late["z34"].advance():
                late["y34"] = ring_y_all(slice(3, 5))
                late["y34"].send()
        if slot == 3:
            late["y2"] = ring_y(2, z)
            late["y2"].send()
        elif slot in (4, 5):
            if late["y2"].advance():
                late["z2"] = ring_z_all(2)
                late["z2"].send()
        elif slot == 6:
            late["z2"].advance()

    kvh = 4
    blocks = NZ * NY
    span = blocks * HW
    per = CHUNK // HW
    me, live = z * NY + y, info[0]
    chunks = me // per + 1
    per_g = GROUP * HW // ROWS
    total = kvh * per_g
    s_bufs, p_bufs, w_bufs = (s_even, s_odd), (p_even, p_odd), (w_even, w_odd)
    zper = per // NY

    def tangents(j, _):
        for b in range(per):
            vv = dot(wT[...], gath[0, j * zper + b // NY, b % NY]).astype(BF)
            for g in range(kvh):
                vT[g, 0:HW, pl.ds(pl.multiple_of(j * CHUNK + b * HW, HW), HW)] = vv[g * HW : (g + 1) * HW]
        return 0

    lax.fori_loop(0, chunks, tangents, 0)
    ones = jnp.where(lax.broadcasted_iota(jnp.int32, (16, span), 0) == 0, 1.0, 0.0).astype(BF)
    for g in range(kvh):
        vT[g, HW : HW + 16, :] = ones
    grad[...] = jnp.zeros_like(grad)
    curv_acc[...] = jnp.zeros_like(curv_acc)
    qpos = me * HW + lax.rem(lax.broadcasted_iota(jnp.int32, (1, ROWS), 1), HW)
    liverow = (qpos < live).astype(F32)

    def step(i, even, score, weigh, back, m_prev):
        odd = 1 - even
        if weigh:
            oacc[...] = jnp.zeros_like(oacc)
        q = qT[i] if score else None

        def body(j, mx):
            o = None
            for u in range(CHUNK // SUB):
                us = pl.multiple_of(j * CHUNK + u * SUB, SUB)
                if back:
                    grad[(i - 2) // per_g, :, pl.ds(us, SUB)] += dot(
                        w_bufs[even][...], p_bufs[even][pl.ds(us, SUB), :], NT
                    )
                if score:
                    b = u * (SUB // HW)
                    kc = gath[1 + i // per_g, j * zper + b // NY, b % NY : b % NY + SUB // HW].reshape(SUB, HW)
                    s = dot(kc, q)
                    kpos = us + lax.broadcasted_iota(jnp.int32, (SUB, ROWS), 0)
                    s = jnp.where(kpos <= qpos, s, -1e30)
                    s_bufs[even][pl.ds(us, SUB), :] = s
                    mx = jnp.maximum(mx, jnp.max(s.reshape(SUB // 8, 8, ROWS), axis=0))
                if weigh:
                    p = jnp.exp2(s_bufs[odd][pl.ds(us, SUB), :] - m_prev).astype(BF)
                    p_bufs[odd][pl.ds(us, SUB), :] = p
                    t = dot(vT[(i - 1) // per_g, :, pl.ds(us, SUB)], p)
                    o = t if o is None else o + t
            if weigh:
                oacc[...] += o
            return mx

        mx = lax.fori_loop(0, chunks, body, jnp.full((8, ROWS), -1e30, F32))
        if weigh:
            o = oacc[...]
            inv = 1.0 / o[HW : HW + 1]
            out = o[0:HW] * inv * liverow
            curv_acc[...] += jnp.sum((out * out).reshape(HW // 8, 8, ROWS), axis=0)
            w_bufs[odd][...] = (out * inv).astype(BF)
        return jnp.max(mx, axis=0, keepdims=True)

    top = step(0, 0, True, False, False, None)
    late["z2"].advance()
    top = step(1, 1, True, True, False, top)
    late["z2"].advance()

    def pair(i, top):
        @pl.when(i == 2)
        def _():
            late["z2"].receive()

        @pl.when(i == 3)
        def _():
            late["y34"].step = 1
            late["y34"].advance()

        @pl.when(i == 4)
        def _():
            late["y34"].step = 2
            late["y34"].receive()

        top = step(2 * i, 0, True, True, True, top)
        return step(2 * i + 1, 1, True, True, True, top)

    top = lax.fori_loop(1, total // 2, pair, top)
    step(total, 0, False, True, True, top)
    step(total + 1, 1, False, False, True, None)

    mixed_ref[...] = jnp.zeros_like(mixed_ref)
    upT_ref[...] = jnp.zeros_like(upT_ref)

    def finish(j, _):
        ks = pl.multiple_of(j * CHUNK, CHUNK)
        grads = [grad[g, :, pl.ds(ks, CHUNK)].astype(BF) for g in range(kvh)]
        mixed = sum(dot(up[:, g * HW : (g + 1) * HW], grads[g]) for g in range(kvh)).astype(BF)
        for b in range(per):
            cols = slice(b * HW, (b + 1) * HW)
            mixed_ref[j * zper + b // NY, b % NY] = mixed[:, cols]
            act = gath[0, j * zper + b // NY, b % NY, 0:RANK, :]
            for g in range(kvh):
                upT_ref[g * HW : (g + 1) * HW, :] += dot(grads[g][:, cols], act, NT)
        return 0

    lax.fori_loop(0, chunks, finish, 0)
    both = curv_acc[:, 0:HW] + curv_acc[:, HW : 2 * HW]
    row = lax.broadcasted_iota(jnp.int32, (8, HW), 0)
    lane = lax.broadcasted_iota(jnp.int32, (8, HW), 1)
    mine = ((me * HW + lane) < live).astype(F32)
    curv_ref[...] = jnp.where(
        row == 0, jnp.sum(both, axis=0, keepdims=True), jnp.where(row == 1, mine, 0.0)
    )
    for flow in made:
        flow.drain()


def attention(info, hidden, queries, keys, down, direction, cosine, sine, wT, up):
    span = NZ * NY * HW
    return pl.pallas_call(
        attend_kernel,
        out_shape=(
            jax.ShapeDtypeStruct((NZ, NY, RANK, HW), BF),
            jax.ShapeDtypeStruct((4 * HW, RANK), F32),
            jax.ShapeDtypeStruct((8, HW), F32),
        ),
        in_specs=[SM] + [VM] * 9,
        out_specs=(VM, VM, VM),
        scratch_shapes=[
            pltpu.VMEM((5, NZ, NY, HW, HW), BF),
            pltpu.VMEM((queries.shape[1] // ROWS, HW, ROWS), BF),
            pltpu.VMEM((span, ROWS), F32),
            pltpu.VMEM((span, ROWS), F32),
            pltpu.VMEM((span, ROWS), BF),
            pltpu.VMEM((span, ROWS), BF),
            pltpu.VMEM((4, HW + 16, span), BF),
            pltpu.VMEM((4, HW, span), F32),
            pltpu.VMEM((HW + 16, ROWS), F32),
            pltpu.VMEM((HW, ROWS), BF),
            pltpu.VMEM((HW, ROWS), BF),
            pltpu.VMEM((8, ROWS), F32),
            pltpu.SemaphoreType.DMA((18, 4, 2)),
            pltpu.SemaphoreType.DMA((18, 4, 2)),
        ],
        compiler_params=pltpu.CompilerParams(
            collective_id=0, has_side_effects=True, vmem_limit_bytes=56 * 1024 * 1024
        ),
    )(info, hidden, queries, keys, down, direction, cosine, sine, wT, up)


def reduce_kernel(
    mixed, upT, curv, hidden, direction, up_direction, down_out, up_out, curv_out,
    got_y, sum_y, got_z, part, got_core, sum_core, got_xy, ups, got_uy, sum_dy, got_dz, all_dp,
    send_sem, recv_sem,
):
    z, y = place()
    ctx = lax.axis_index("ctx")
    dp = lax.axis_index("dp")
    x, core = dp // 2, lax.rem(dp, 2)
    barrier = pltpu.get_barrier_semaphore()

    def at_y(o):
        return {"ctx": z * NY + lax.rem(y + o, NY)}

    def at_z(o):
        return {"ctx": lax.rem(z + o, NZ) * NY + y}

    def at_dp(o):
        return {"dp": lax.rem(dp + o, 8)}

    def at_xy(ox, oy):
        return {"dp": lax.rem(x + ox, NX) * 2 + core, "ctx": z * NY + lax.rem(y + oy, NY)}

    plane = [(ox, oy) for ox in range(NX) for oy in range(NY) if ox or oy]
    for ox, oy in plane:
        pl.semaphore_signal(barrier, inc=1, device_id=at_xy(ox, oy), device_id_type=MESH)
    for o in range(1, NZ):
        pl.semaphore_signal(barrier, inc=1, device_id=at_z(o), device_id_type=MESH)
    for o in range(NX):
        other = {"dp": lax.rem(x + o, NX) * 2 + 1 - core}
        pl.semaphore_signal(barrier, inc=1, device_id=other, device_id_type=MESH)

    used = [0]
    sent = []

    def send(src, dst, to):
        copy = pltpu.make_async_remote_copy(
            src_ref=src, dst_ref=dst, send_sem=send_sem.at[used[0]], recv_sem=recv_sem.at[used[0]],
            device_id=to, device_id_type=MESH,
        )
        used[0] += 1
        copy.start()
        sent.append(copy)
        return copy

    pl.semaphore_wait(barrier, 26)

    copies = [
        send(mixed.at[:, lax.rem(y + o, NY)], got_y.at[o - 1], at_y(o)) for o in range(1, NY)
    ]
    for i in range(32):
        block = upT[16 * i : 16 * i + 16, :]
        ups[i % NY, i // NY] = jnp.concatenate([block[0:8], block[8:16]], axis=1)
    for i in range(NY):
        ups[i, NZ] = curv[...]

    def squares(i, acc):
        d = direction[:, pl.ds(pl.multiple_of(i * 512, 512), 512)].astype(F32)
        return acc + jnp.sum((d * d).reshape(8, 8, 512), axis=0)

    squared = jnp.sum(lax.fori_loop(0, 16, squares, jnp.zeros((8, 512), F32)))
    ud = up_direction[...].astype(F32)
    squared = squared + jnp.sum(ud * ud)

    for copy in copies:
        copy.wait_recv()

    def add_y(i, _):
        acc = mixed[i, y].astype(F32)
        for o in range(NY - 1):
            acc = acc + got_y[o, i].astype(F32)
        sum_y[i] = acc.astype(BF)
        return 0

    lax.fori_loop(0, NZ, add_y, 0)
    copies = [
        send(sum_y.at[lax.rem(z + o, NZ)], got_z.at[o - 1], at_z(o)) for o in range(1, NZ)
    ]
    for copy in copies:
        copy.wait_recv()
    own = sum_y[z].astype(F32)
    for o in range(NZ - 1):
        own = own + got_z[o].astype(F32)
    own = own.astype(BF)

    def down(i, _):
        d = dot(own, hidden[:, pl.ds(pl.multiple_of(i * 256, 256), 256)])
        for r in range(8):
            rows = d[8 * r : 8 * r + 8]
            part[r // 2, r % 2, i] = jnp.concatenate([rows[:, 0:HW], rows[:, HW:]], axis=0).astype(BF)
        return 0

    lax.fori_loop(0, 32, down, 0)

    copy = send(part.at[:, 1 - core], got_core, {"dp": x * 2 + 1 - core})
    copy.wait_recv()

    def add_core(i, _):
        for xx in range(NX):
            sum_core[xx, i % NY, i // NY] = (part[xx, core, i].astype(F32) + got_core[xx, i].astype(F32)).astype(BF)
        return 0

    lax.fori_loop(0, 32, add_core, 0)
    copies = []
    for k, (ox, oy) in enumerate(plane):
        copies.append(
            send(sum_core.at[lax.rem(x + ox, NX), lax.rem(y + oy, NY)], got_xy.at[k], at_xy(ox, oy))
        )
    for o in range(1, NY):
        copies.append(send(ups.at[lax.rem(y + o, NY)], got_uy.at[o - 1], at_y(o)))
    for copy in copies:
        copy.wait_recv()
    scal = ups[y, NZ]
    for o in range(NY - 1):
        scal = scal + got_uy[o, NZ]
    for i in range(NZ):
        acc = sum_core[x, y, i].astype(F32)
        for k in range(len(plane)):
            acc = acc + got_xy[k, i].astype(F32)
        upa = ups[y, i]
        for o in range(NY - 1):
            upa = upa + got_uy[o, i]
        sum_dy[i, 0:16] = acc
        sum_dy[i, 16:24] = upa
        sum_dy[i, 24:32] = scal
    copies = [
        send(sum_dy.at[lax.rem(z + o, NZ)], got_dz.at[o - 1], at_z(o)) for o in range(1, NZ)
    ]
    for copy in copies:
        copy.wait_recv()
    acc = sum_dy[z]
    for o in range(NZ - 1):
        acc = acc + got_dz[o]
    all_dp[dp] = acc
    copies = [send(all_dp.at[dp], all_dp.at[dp], at_dp(o)) for o in range(1, 8)]
    for o in range(1, 8):
        slot = lax.rem(dp + 8 - o, 8)
        base = used[0] - 7 + o - 1
        pltpu.make_async_remote_copy(
            src_ref=all_dp.at[slot], dst_ref=all_dp.at[slot], send_sem=send_sem.at[base],
            recv_sem=recv_sem.at[base], device_id=at_dp(o), device_id_type=MESH,
        ).wait_recv()
    tail = all_dp[0, 16:32]
    for r in range(1, 8):
        tail = tail + all_dp[r, 16:32]
    curv_sum = jnp.sum(tail[8:9])
    count = jnp.sum(tail[9:10])
    rescale = squared / (curv_sum + 1e-06)
    for r in range(8):
        down_out[8 * r : 8 * r + 8, 0:HW] = all_dp[r, 0:8] * rescale
        down_out[8 * r : 8 * r + 8, HW : 2 * HW] = all_dp[r, 8:16] * rescale
    up_out[0:8, :] = tail[0:8, 0:RANK] * rescale
    up_out[8:16, :] = tail[0:8, RANK:HW] * rescale
    curv_out[...] = jnp.full((8, HW), curv_sum / count, F32)
    for copy in sent:
        copy.wait_send()


def reduce(mixed, upT, curv, hidden, direction, up_direction):
    return pl.pallas_call(
        reduce_kernel,
        out_shape=(
            jax.ShapeDtypeStruct((RANK, 256), F32),
            jax.ShapeDtypeStruct((16, RANK), F32),
            jax.ShapeDtypeStruct((8, HW), F32),
        ),
        in_specs=[VM] * 6,
        out_specs=(VM, VM, VM),
        scratch_shapes=[
            pltpu.VMEM((NY - 1, NZ, RANK, HW), BF),
            pltpu.VMEM((NZ, RANK, HW), BF),
            pltpu.VMEM((NZ - 1, RANK, HW), BF),
            pltpu.VMEM((NX, 2, 32, 16, HW), BF),
            pltpu.VMEM((NX, 32, 16, HW), BF),
            pltpu.VMEM((NX, NY, NZ, 16, HW), BF),
            pltpu.VMEM((NX * NY - 1, NZ, 16, HW), BF),
            pltpu.VMEM((NY, NZ + 1, 8, HW), F32),
            pltpu.VMEM((NY - 1, NZ + 1, 8, HW), F32),
            pltpu.VMEM((NZ, 32, HW), F32),
            pltpu.VMEM((NZ - 1, 32, HW), F32),
            pltpu.VMEM((8, 32, HW), F32),
            pltpu.SemaphoreType.DMA((43,)),
            pltpu.SemaphoreType.DMA((43,)),
        ],
        compiler_params=pltpu.CompilerParams(
            collective_id=1, has_side_effects=True, vmem_limit_bytes=48 * 1024 * 1024
        ),
    )(mixed, upT, curv, hidden, direction, up_direction)


def body(hidden, queries, keys, down, up, direction, up_direction, window, lengths):
    seq = hidden.shape[1]
    span = seq * NZ * NY
    ctx = lax.axis_index("ctx")
    position = window[0] * span + ctx * seq + jnp.arange(seq, dtype=jnp.int32)
    inv_freq = jnp.exp(jnp.arange(HW // 2, dtype=F32) * (-2.0 * math.log(1000000.0) / HW))
    angles = position.astype(F32)[:, None] * inv_freq
    cosine, sine = jnp.cos(angles), jnp.sin(angles)
    cosine = jnp.concatenate([cosine, cosine], axis=1)
    sine = jnp.concatenate([-sine, sine], axis=1)
    info = (lengths - window * span).astype(jnp.int32)
    wT = jnp.concatenate([up_direction, up], axis=0).T
    mixed, upT, curv = attention(
        info, hidden[0], queries[0], keys[0], down.T, direction.T, cosine, sine, wT, up
    )
    down_out, up_out, curv_out = reduce(mixed, upT, curv, hidden[0], direction.T, up_direction)
    return down_out.T, up_out.T, curv_out[0, 0]


def solution(mesh):
    placed = (
        P("dp", "ctx", None),
        P("dp", "ctx", None),
        P("dp", "ctx", None),
        P(),
        P(),
        P(),
        P(),
        P("dp"),
        P("dp"),
    )
    return jax.shard_map(
        body,
        mesh=mesh,
        in_specs=placed,
        out_specs=(P("ctx", None), P(None, "ctx"), P()),
        check_vma=False,
    )
```

time: 158 us -> 137 us (0.87)
  Pallas kernels: 142 us -> 127 us
  local copies, waits for them, and re-layouts: 11.9 us -> 6.33 us
    pallas_call x1, Pallas kernels: 69.9 us -> 59.5 us  [reduce(): pl.pallas_call(reduce_kernel, out_shape=(jax.ShapeDtypeStruct((RANK, 256)...]
    unnamed x26 -> x16, local copies, waits for them, and re-layouts: 11.4 us -> 5.81 us
    pallas_call x2 -> x1, Pallas kernels: 71.8 us -> 67.5 us  [attention(): pl.pallas_call(attend_kernel, out_shape=(jax.ShapeDtypeStruct((NZ, NY, RA...]
where the time goes in v2:
time: 137 us
  Pallas kernels  127 us (93%)
  local copies, waits for them, and re-layouts  6.33 us (5%)
  between operations  2.01 us (1%)
  other arithmetic  1.84 us (1%)
    pallas_call x1, Pallas kernels, attention(): pl.pallas_call(attend_kernel, out_shape=(jax.ShapeDtypeStruct((NZ, NY, RA...  67.5 us
    pallas_call x1, Pallas kernels, reduce(): pl.pallas_call(reduce_kernel, out_shape=(jax.ShapeDtypeStruct((RANK, 256)...  59.5 us
    unnamed x16, local copies, waits for them, and re-layouts  5.81 us

profile of v2, /device:TPU:1, one launch (start us, length us, event | category | flops | bytes accessed | tf_op | source)
XLA Modules:
  0.0 137.2 jit_solution(16479826332720481363)
XLA Ops:
  2.0 1.0 copy.13
  2.9 1.0 copy.12
  3.9 0.8 maximum_bitcast_fusion.wT
  4.7 0.3 fusion
  5.0 0.8 pad_maximum_fusion
  5.7 0.0 copy-start
  5.7 0.0 copy-start.1
  5.7 0.0 copy-start.3
  5.7 67.5 %shard_map.112 = (bf16[8,4,64,128]{3,2,1,0:T(8,128)(2,1)}, f32[512,64]{1,0:T(8,128)}, f32[8,128]{1,0:T(8,128)}) custom-call(s32[1]{0:T(128)S(6)} %sub.3.info, bf16[128,8192]{1,0:T(8,128)(2,1)} %bitcast.11, bf16[128,4096]{1,0:T(8,128)(2,1)} %bitcast.17, bf16[128,512]{1,0:T(8,128)(2,1)} %bitcast.19, bf16[64,8192]{1,0:T(8,128)(2,1)} %bitcast.18, ...), custom_call_target="tpu_custom_call" | custom-call | tf_op jit(solution)/shard_map/pallas_call | solution.py:321
  73.2 0.0 copy-done
  73.3 0.0 copy-done.1
  73.3 0.0 copy-done.3
  73.3 0.0 copy-start.2
  73.3 1.0 copy-done.2
  74.3 0.0 copy-start.4
  74.3 0.9 copy-done.4
  75.3 0.0 copy-start.5
  75.3 0.7 copy-done.5
  75.9 59.5 %shard_map.113 = (f32[64,256]{1,0:T(8,128)S(1)}, f32[16,64]{1,0:T(8,128)S(1)}, f32[8,128]{1,0:T(8,128)S(1)}) custom-call(bf16[8,4,64,128]{3,2,1,0:T(8,128)(2,1)S(1)} %copy-done.2, f32[512,64]{1,0:T(8,128)S(1)} %copy-done.4, f32[8,128]{1,0:T(8,128)S(1)} %copy-done.5, bf16[128,8192]{1,0:T(8,128)(2,1)S(1)} %bitcast.12, bf16[64,8192]{1,0:T(8,128)(2,1)S(1)} %bitcast.14, ...), custom_call_target="tpu_custom_call" | custom-call | tf_op jit(solution)/shard_map/pallas_call | solution.py:511
  135.5 0.5 slice.3
  136.0 0.6 copy.18
  136.6 0.6 copy.19
  (2 shorter events, 0.0 us)
Async XLA Ops:
  5.7 67.5 %copy-start = (bf16[1,128,8192]{2,1,0:T(8,128)(2,1)S(1)}, bf16[1,128,8192]{2,1,0:T(8,128)(2,1)}, u32[]{:S(2)}) copy-start(bf16[1,128,8192]{2,1,0:T(8,128)(2,1)} %param.9) | copy-start | bytes 6291460
  5.7 67.5 %copy-start.1 = (bf16[8192,64]{0,1:T(8,128)(2,1)S(1)}, bf16[8192,64]{0,1:T(8,128)(2,1)}, u32[]{:S(2)}) copy-start(bf16[8192,64]{0,1:T(8,128)(2,1)} %param.14) | copy-start | bytes 3145732
  5.7 67.5 %copy-start.3 = (bf16[64,512]{1,0:T(8,128)(2,1)S(1)}, bf16[64,512]{1,0:T(8,128)(2,1)}, u32[]{:S(2)}) copy-start(bf16[64,512]{1,0:T(8,128)(2,1)} %up_direction.1) | copy-start | bytes 196612
  73.3 1.0 copy-start.2
  74.3 0.9 copy-start.4
  75.3 0.7 copy-start.5

commit v3 on v2

v3 whole, which is shorter than its diff:
```python
import functools
import math

import jax
import jax.numpy as jnp
from jax import lax
from jax.experimental import pallas as pl
from jax.experimental.pallas import tpu as pltpu
from jax.sharding import PartitionSpec as P

HW = 128
GROUP = 8
RANK = 64
NZ, NY, NX = 8, 4, 4
ROWS = 256
CHUNK = 2048
SUB = 256
F32 = jnp.float32
BF = jnp.bfloat16
MESH = pl.DeviceIdType.MESH
NN = (((1,), (0,)), ((), ()))
NT = (((1,), (1,)), ((), ()))
VM = pl.BlockSpec(memory_space=pltpu.VMEM)
SM = pl.BlockSpec(memory_space=pltpu.SMEM)


def dot(a, b, dims=NN):
    return lax.dot_general(a, b, dims, preferred_element_type=F32)


def place():
    ctx = lax.axis_index("ctx")
    return ctx // NY, lax.rem(ctx, NY)


def forward(size):
    steps = [[(-k, 1, None), (k, -1, None)] for k in range(size // 2 - 1)]
    last = size // 2 - 1
    return steps + [[(-last, 1, 0), (last, -1, 1)]]


DIRECT4 = [[(0, 1, None), (0, -1, None), (0, 2, None)]]
THREE8 = [
    [(0, 1, None), (0, -1, None)],
    [(-1, 1, None), (1, -1, None)],
    [(-2, 1, None), (2, -1, None), (-2, 2, 0), (2, -2, 1)],
]
TWO8 = [
    [(0, 1, None), (0, -1, None), (0, 2, None), (0, -2, None)],
    [(-2, 1, None), (2, -1, None), (-2, 2, 0), (2, -2, 1)],
]


class Flow:
    def __init__(self, index, size, here, plan, block, peer, sems):
        self.index, self.size, self.here, self.plan = index, size, here, plan
        self.block, self.peer = block, peer
        self.send_sem, self.recv_sem = sems
        self.step = -1

    def copy(self, step, k, arriving):
        held, hop, half = self.plan[step][k]
        origin = held - hop if arriving else held
        ref = self.block(lax.rem(self.here + origin + 2 * self.size, self.size), half)
        return pltpu.make_async_remote_copy(
            src_ref=ref,
            dst_ref=ref,
            send_sem=self.send_sem.at[self.index, step, k],
            recv_sem=self.recv_sem.at[self.index, step, k],
            device_id=self.peer(lax.rem(self.here + hop + self.size, self.size)),
            device_id_type=MESH,
        )

    def send(self, step):
        self.step = step
        for k in range(len(self.plan[step])):
            self.copy(step, k, False).start()

    def receive(self, step):
        for k in range(len(self.plan[step])):
            self.copy(step, k, True).wait_recv()
        return sorted({(held - hop) % self.size for held, hop, _ in self.plan[step]})

    def advance(self):
        step = self.step
        came = self.receive(step)
        end = step + 1 == len(self.plan)
        if not end:
            self.send(step + 1)
        return came, end

    def drain(self):
        for step, moves in enumerate(self.plan):
            for k in range(len(moves)):
                self.copy(step, k, False).wait_send()


def cut(ref, half, axis):
    if half is None:
        return ref
    return ref.at[(slice(None),) * axis + (pl.ds(half * 64, 64),)]


def fisher_kernel(
    info, hidden_any, queries_any, keys, down_any, direction_any, up_direction, cosine, sine, wT, up,
    down_out, up_out, curv_out,
    hidden, queries, down, direction, load_sem,
    gath, qT, s_even, s_odd, p_even, p_odd, vT, act, grad, oacc, w_even, w_odd, curv_acc, mixed, upT,
    got_y, sum_y, got_z, part, got_core, sum_core, got_xy, ups, got_uy, sum_dy, got_dz, all_dp,
    gsend, grecv, send_sem, recv_sem,
):
    z, y = place()
    dp = lax.axis_index("dp")
    x, core = dp // 2, lax.rem(dp, 2)
    loads = [
        pltpu.make_async_copy(src, dst, load_sem.at[k])
        for k, (src, dst) in enumerate(
            ((hidden_any, hidden), (down_any, down), (direction_any, direction), (queries_any, queries))
        )
    ]
    for copy in loads:
        copy.start()
    barrier = pltpu.get_barrier_semaphore()

    def at(zz, yy):
        return {"ctx": zz * NY + yy}

    def at_y(o):
        return {"ctx": z * NY + lax.rem(y + o, NY)}

    def at_z(o):
        return {"ctx": lax.rem(z + o, NZ) * NY + y}

    def at_dp(o):
        return {"dp": lax.rem(dp + o, 8)}

    def at_xy(ox, oy):
        return {"dp": lax.rem(x + ox, NX) * 2 + core, "ctx": z * NY + lax.rem(y + oy, NY)}

    plane = [(ox, oy) for ox in range(NX) for oy in range(NY) if ox or oy]
    for ox, oy in plane:
        pl.semaphore_signal(barrier, inc=1, device_id=at_xy(ox, oy), device_id_type=MESH)
    for o in range(1, NZ):
        pl.semaphore_signal(barrier, inc=1, device_id=at_z(o), device_id_type=MESH)
    for o in range(NX):
        other = {"dp": lax.rem(x + o, NX) * 2 + 1 - core}
        pl.semaphore_signal(barrier, inc=1, device_id=other, device_id_type=MESH)

    ys = [lax.rem(y + o, NY) for o in range(NY)]
    zs = [lax.rem(z + o, NZ) for o in range(NZ)]
    cos, sin = cosine[...], sine[...]

    def turn(u):
        u = u.astype(F32)
        return u * cos + pltpu.roll(u, HW // 2, 1) * sin

    for g in range(4):
        gath[1 + g, z, y] = turn(keys[:, g * HW : (g + 1) * HW]).astype(BF)
    for copy in loads[:3]:
        copy.wait()
    gath[0, z, y, 0:RANK, :] = dot(down[...], hidden[...], NT).astype(BF)
    gath[0, z, y, RANK:HW, :] = dot(direction[...], hidden[...], NT).astype(BF)
    pl.semaphore_wait(barrier, 26)

    made = []
    sems = (gsend, grecv)

    def ring_y(plan, block):
        made.append(Flow(len(made), NY, y, plan, block, lambda to: at(z, to), sems))
        return made[-1]

    def ring_z(plan, block):
        made.append(Flow(len(made), NZ, z, plan, block, lambda to: at(to, y), sems))
        return made[-1]

    def y_lane(head, zz, plan):
        return ring_y(plan, lambda o, half: cut(gath.at[head, zz, o], half, 0))

    def z_lane(head, yy, plan):
        return ring_z(plan, lambda o, half: cut(gath.at[head, o, yy], half, 0))

    first_y, first_z = y_lane(0, z, DIRECT4), z_lane(1, y, TWO8)
    act_lanes = {0: z_lane(0, y, forward(NZ))}
    key_lanes = [y_lane(1, z, forward(NY))]
    for flow in (first_z, key_lanes[0], first_y, act_lanes[0]):
        flow.send(0)

    loads[3].wait()
    scale = math.log2(math.e) / math.sqrt(HW)

    def rotate_queries(i, _):
        for h in range(ROWS // HW):
            u = queries[:, pl.ds(pl.multiple_of(i * ROWS + h * HW, HW), HW)]
            qT[i, :, h * HW : (h + 1) * HW] = jnp.transpose(turn(u) * scale).astype(BF)
        return 0

    lax.fori_loop(0, qT.shape[0], rotate_queries, 0)

    kvh = 4
    blocks = NZ * NY
    span = blocks * HW
    per = CHUNK // HW
    me, live = z * NY + y, info[0]
    chunks = me // per + 1
    per_g = GROUP * HW // ROWS
    total = kvh * per_g
    zper = per // NY

    def tangents(zz, yy):
        cols = pl.ds(pl.multiple_of((zz * NY + yy) * HW, HW), HW)
        vv = dot(wT[...], gath[0, zz, yy]).astype(BF)
        for g in range(kvh):
            vT[g, 0:HW, cols] = vv[g * HW : (g + 1) * HW]
        act[:, cols] = gath[0, zz, yy, 0:RANK, :]

    tangents(z, y)
    ones = jnp.where(lax.broadcasted_iota(jnp.int32, (16, span), 0) == 0, 1.0, 0.0).astype(BF)
    for g in range(kvh):
        vT[g, HW : HW + 16, :] = ones
    grad[...] = jnp.zeros_like(grad)
    curv_acc[...] = jnp.zeros_like(curv_acc)

    for slot in range(1, 5):
        new_keys, new_acts, landed = [], {}, []
        if slot <= 2:
            came, _ = first_z.advance()
            new_keys = [y_lane(1, zs[o], forward(NY) if slot == 1 else DIRECT4) for o in came]
        for flow in list(key_lanes):
            if flow.advance()[1]:
                key_lanes.remove(flow)
        for flow in new_keys:
            flow.send(0)
        key_lanes += new_keys
        if slot == 1:
            came, _ = first_y.advance()
            new_acts = {o: z_lane(0, ys[o], THREE8) for o in came}
            landed += [(0, o) for o in came]
        for o, flow in list(act_lanes.items()):
            came, end = flow.advance()
            landed += [(oz, o) for oz in came]
            if end:
                del act_lanes[o]
        for flow in new_acts.values():
            flow.send(0)
        act_lanes.update(new_acts)
        if slot == 2:
            keys2_y = y_lane(2, z, DIRECT4)
            keys2_y.send(0)
            keys34_z = ring_z(THREE8, lambda o, half: cut(gath.at[3:5, o, y], half, 1))
            keys34_z.send(0)
        if slot == 3:
            keys2_y.receive(0)
            keys2_z = ring_z(THREE8, lambda o, half: cut(gath.at[2, o], half, 1))
            keys2_z.send(0)
            keys34_z.advance()
        if slot == 4:
            keys2_z.advance()
            keys34_z.advance()
        for oz, oy in landed:
            tangents(zs[oz], ys[oy])
    assert not key_lanes and not act_lanes

    s_bufs, p_bufs, w_bufs = (s_even, s_odd), (p_even, p_odd), (w_even, w_odd)
    qpos = me * HW + lax.rem(lax.broadcasted_iota(jnp.int32, (1, ROWS), 1), HW)
    liverow = (qpos < live).astype(F32)

    def step(i, even, score, weigh, back, m_prev):
        odd = 1 - even
        if weigh:
            oacc[...] = jnp.zeros_like(oacc)
        q = qT[i] if score else None

        def body(j, mx):
            o = None
            for u in range(CHUNK // SUB):
                us = pl.multiple_of(j * CHUNK + u * SUB, SUB)
                if back:
                    grad[(i - 2) // per_g, :, pl.ds(us, SUB)] += dot(
                        w_bufs[even][...], p_bufs[even][pl.ds(us, SUB), :], NT
                    )
                if score:
                    b = u * (SUB // HW)
                    kc = gath[1 + i // per_g, j * zper + b // NY, b % NY : b % NY + SUB // HW].reshape(SUB, HW)
                    s = dot(kc, q)
                    kpos = us + lax.broadcasted_iota(jnp.int32, (SUB, ROWS), 0)
                    s = jnp.where(kpos <= qpos, s, -1e30)
                    s_bufs[even][pl.ds(us, SUB), :] = s
                    mx = jnp.maximum(mx, jnp.max(s.reshape(SUB // 8, 8, ROWS), axis=0))
                if weigh:
                    p = jnp.exp2(s_bufs[odd][pl.ds(us, SUB), :] - m_prev).astype(BF)
                    p_bufs[odd][pl.ds(us, SUB), :] = p
                    t = dot(vT[(i - 1) // per_g, :, pl.ds(us, SUB)], p)
                    o = t if o is None else o + t
            if weigh:
                oacc[...] += o
            return mx

        mx = lax.fori_loop(0, chunks, body, jnp.full((8, ROWS), -1e30, F32))
        if weigh:
            o = oacc[...]
            inv = 1.0 / o[HW : HW + 1]
            out = o[0:HW] * inv * liverow
            curv_acc[...] += jnp.sum((out * out).reshape(HW // 8, 8, ROWS), axis=0)
            w_bufs[odd][...] = (out * inv).astype(BF)
        return jnp.max(mx, axis=0, keepdims=True)

    def y_rest(head):
        return ring_y(forward(NY), lambda o, half: cut(gath.at[head, :, o], half, 1))

    top = step(0, 0, True, False, False, None)
    keys2_z.advance()
    keys34_z.advance()
    keys3_y, keys4_y = y_rest(3), y_rest(4)
    keys3_y.send(0)
    keys4_y.send(0)
    top = step(1, 1, True, True, False, top)

    def pair(i, top):
        @pl.when(i == 2)
        def _():
            keys2_z.receive(2)
            keys3_y.receive(0)
            keys3_y.send(1)

        @pl.when(i == 3)
        def _():
            keys4_y.receive(0)
            keys4_y.send(1)

        @pl.when(i == 4)
        def _():
            keys3_y.receive(1)

        @pl.when(i == 6)
        def _():
            keys4_y.receive(1)

        top = step(2 * i, 0, True, True, True, top)
        return step(2 * i + 1, 1, True, True, True, top)

    top = lax.fori_loop(1, total // 2, pair, top)
    step(total, 0, False, True, True, top)
    step(total + 1, 1, False, False, True, None)

    used = [0]
    sent = []

    def send(src, dst, to):
        copy = pltpu.make_async_remote_copy(
            src_ref=src, dst_ref=dst, send_sem=send_sem.at[used[0]], recv_sem=recv_sem.at[used[0]],
            device_id=to, device_id_type=MESH,
        )
        used[0] += 1
        copy.start()
        sent.append(copy)
        return copy

    mixed[...] = jnp.zeros_like(mixed)
    upT[...] = jnp.zeros_like(upT)

    def mix(j, _):
        ks = pl.multiple_of(j * CHUNK, CHUNK)
        acc = sum(
            dot(up[:, g * HW : (g + 1) * HW], grad[g, :, pl.ds(ks, CHUNK)].astype(BF)) for g in range(kvh)
        ).astype(BF)
        for b in range(per):
            mixed[j * zper + b // NY, b % NY] = acc[:, b * HW : (b + 1) * HW]
        return 0

    lax.fori_loop(0, chunks, mix, 0)

    copies = [
        send(mixed.at[:, lax.rem(y + o, NY)], got_y.at[o - 1], at_y(o)) for o in range(1, NY)
    ]

    def ascend(j, _):
        ks = pl.multiple_of(j * CHUNK, CHUNK)
        for g in range(kvh):
            upT[g * HW : (g + 1) * HW, :] += dot(
                grad[g, :, pl.ds(ks, CHUNK)].astype(BF), act[:, pl.ds(ks, CHUNK)], NT
            )
        return 0

    lax.fori_loop(0, chunks, ascend, 0)
    both = curv_acc[:, 0:HW] + curv_acc[:, HW : 2 * HW]
    row = lax.broadcasted_iota(jnp.int32, (8, HW), 0)
    lane = lax.broadcasted_iota(jnp.int32, (8, HW), 1)
    mine = ((me * HW + lane) < live).astype(F32)
    curv = jnp.where(
        row == 0, jnp.sum(both, axis=0, keepdims=True), jnp.where(row == 1, mine, 0.0)
    )
    for i in range(32):
        block = upT[16 * i : 16 * i + 16, :]
        ups[i % NY, i // NY] = jnp.concatenate([block[0:8], block[8:16]], axis=1)
    for i in range(NY):
        ups[i, NZ] = curv

    def squares(i, acc):
        d = direction[:, pl.ds(pl.multiple_of(i * 512, 512), 512)].astype(F32)
        return acc + jnp.sum((d * d).reshape(8, 8, 512), axis=0)

    squared = jnp.sum(lax.fori_loop(0, 16, squares, jnp.zeros((8, 512), F32)))
    ud = up_direction[...].astype(F32)
    squared = squared + jnp.sum(ud * ud)

    for copy in copies:
        copy.wait_recv()

    def add_y(i, _):
        acc = mixed[i, y].astype(F32)
        for o in range(NY - 1):
            acc = acc + got_y[o, i].astype(F32)
        sum_y[i] = acc.astype(BF)
        return 0

    lax.fori_loop(0, NZ, add_y, 0)
    copies = [
        send(sum_y.at[lax.rem(z + o, NZ)], got_z.at[o - 1], at_z(o)) for o in range(1, NZ)
    ]
    for copy in copies:
        copy.wait_recv()
    own = sum_y[z].astype(F32)
    for o in range(NZ - 1):
        own = own + got_z[o].astype(F32)
    own = own.astype(BF)

    def make_down(h):
        def down_block(i, _):
            for u in range(2):
                k = 2 * i + u
                d = dot(own, hidden[:, pl.ds(pl.multiple_of((h * 16 + k) * 256, 256), 256)])
                for r in range(8):
                    rows = d[8 * r : 8 * r + 8]
                    part[h, r // 2, r % 2, k] = jnp.concatenate([rows[:, 0:HW], rows[:, HW:]], axis=0).astype(BF)
            return 0

        lax.fori_loop(0, 8, down_block, 0)
        return send(part.at[h, :, 1 - core], got_core.at[h], {"dp": x * 2 + 1 - core})

    def add_core(h):
        def add(i, _):
            for xx in range(NX):
                sum_core[h, xx, i % NY, i // NY] = (
                    part[h, xx, core, i].astype(F32) + got_core[h, xx, i].astype(F32)
                ).astype(BF)
            return 0

        lax.fori_loop(0, 16, add, 0)
        return [
            send(
                sum_core.at[h, lax.rem(x + ox, NX), lax.rem(y + oy, NY)], got_xy.at[h, k], at_xy(ox, oy)
            )
            for k, (ox, oy) in enumerate(plane)
        ]

    cores = [make_down(0), make_down(1)]
    cores[0].wait_recv()
    first = add_core(0)
    up_copies = [send(ups.at[lax.rem(y + o, NY)], got_uy.at[o - 1], at_y(o)) for o in range(1, NY)]
    cores[1].wait_recv()
    second = add_core(1)
    for h, copies in ((0, first), (1, second)):
        for copy in copies:
            copy.wait_recv()
        for i in range(NZ // 2):
            acc = sum_core[h, x, y, i].astype(F32)
            for k in range(len(plane)):
                acc = acc + got_xy[h, k, i].astype(F32)
            sum_dy[h * (NZ // 2) + i, 0:16] = acc
    for copy in up_copies:
        copy.wait_recv()
    scal = ups[y, NZ]
    for o in range(NY - 1):
        scal = scal + got_uy[o, NZ]
    for i in range(NZ):
        upa = ups[y, i]
        for o in range(NY - 1):
            upa = upa + got_uy[o, i]
        sum_dy[i, 16:24] = upa
        sum_dy[i, 24:32] = scal
    copies = [
        send(sum_dy.at[lax.rem(z + o, NZ)], got_dz.at[o - 1], at_z(o)) for o in range(1, NZ)
    ]
    for copy in copies:
        copy.wait_recv()
    acc = sum_dy[z]
    for o in range(NZ - 1):
        acc = acc + got_dz[o]
    all_dp[dp] = acc
    copies = [send(all_dp.at[dp], all_dp.at[dp], at_dp(o)) for o in range(1, 8)]
    for o in range(1, 8):
        slot = lax.rem(dp + 8 - o, 8)
        base = used[0] - 7 + o - 1
        pltpu.make_async_remote_copy(
            src_ref=all_dp.at[slot], dst_ref=all_dp.at[slot], send_sem=send_sem.at[base],
            recv_sem=recv_sem.at[base], device_id=at_dp(o), device_id_type=MESH,
        ).wait_recv()
    tail = all_dp[0, 16:32]
    for r in range(1, 8):
        tail = tail + all_dp[r, 16:32]
    curv_sum = jnp.sum(tail[8:9])
    count = jnp.sum(tail[9:10])
    rescale = squared / (curv_sum + 1e-06)
    for r in range(8):
        down_out[8 * r : 8 * r + 8, 0:HW] = all_dp[r, 0:8] * rescale
        down_out[8 * r : 8 * r + 8, HW : 2 * HW] = all_dp[r, 8:16] * rescale
    up_out[0:8, :] = tail[0:8, 0:RANK] * rescale
    up_out[8:16, :] = tail[0:8, RANK:HW] * rescale
    curv_out[...] = jnp.full((8, HW), curv_sum / count, F32)
    for flow in made:
        flow.drain()
    for copy in sent:
        copy.wait_send()


def fisher(info, hidden, queries, keys, down, direction, up_direction, cosine, sine, wT, up):
    span = NZ * NY * HW
    half = NZ // 2
    anywhere = pl.BlockSpec(memory_space=pl.ANY)
    return pl.pallas_call(
        fisher_kernel,
        out_shape=(
            jax.ShapeDtypeStruct((RANK, 256), F32),
            jax.ShapeDtypeStruct((16, RANK), F32),
            jax.ShapeDtypeStruct((8, HW), F32),
        ),
        in_specs=[SM, anywhere, anywhere, VM, anywhere, anywhere, VM, VM, VM, VM, VM],
        out_specs=(VM, VM, VM),
        scratch_shapes=[
            pltpu.VMEM(hidden.shape, BF),
            pltpu.VMEM(queries.shape, BF),
            pltpu.VMEM(down.shape, BF),
            pltpu.VMEM(direction.shape, BF),
            pltpu.SemaphoreType.DMA((4,)),
            pltpu.VMEM((5, NZ, NY, HW, HW), BF),
            pltpu.VMEM((queries.shape[1] // ROWS, HW, ROWS), BF),
            pltpu.VMEM((span, ROWS), F32),
            pltpu.VMEM((span, ROWS), F32),
            pltpu.VMEM((span, ROWS), BF),
            pltpu.VMEM((span, ROWS), BF),
            pltpu.VMEM((4, HW + 16, span), BF),
            pltpu.VMEM((RANK, span), BF),
            pltpu.VMEM((4, HW, span), F32),
            pltpu.VMEM((HW + 16, ROWS), F32),
            pltpu.VMEM((HW, ROWS), BF),
            pltpu.VMEM((HW, ROWS), BF),
            pltpu.VMEM((8, ROWS), F32),
            pltpu.VMEM((NZ, NY, RANK, HW), BF),
            pltpu.VMEM((4 * HW, RANK), F32),
            pltpu.VMEM((NY - 1, NZ, RANK, HW), BF),
            pltpu.VMEM((NZ, RANK, HW), BF),
            pltpu.VMEM((NZ - 1, RANK, HW), BF),
            pltpu.VMEM((2, NX, 2, 16, 16, HW), BF),
            pltpu.VMEM((2, NX, 16, 16, HW), BF),
            pltpu.VMEM((2, NX, NY, half, 16, HW), BF),
            pltpu.VMEM((2, NX * NY - 1, half, 16, HW), BF),
            pltpu.VMEM((NY, NZ + 1, 8, HW), F32),
            pltpu.VMEM((NY - 1, NZ + 1, 8, HW), F32),
            pltpu.VMEM((NZ, 32, HW), F32),
            pltpu.VMEM((NZ - 1, 32, HW), F32),
            pltpu.VMEM((8, 32, HW), F32),
            pltpu.SemaphoreType.DMA((19, 4, 4)),
            pltpu.SemaphoreType.DMA((19, 4, 4)),
            pltpu.SemaphoreType.DMA((59,)),
            pltpu.SemaphoreType.DMA((59,)),
        ],
        compiler_params=pltpu.CompilerParams(
            collective_id=0, has_side_effects=True, vmem_limit_bytes=58 * 1024 * 1024
        ),
    )(info, hidden, queries, keys, down, direction, up_direction, cosine, sine, wT, up)


def body(hidden, queries, keys, down, up, direction, up_direction, window, lengths):
    seq = hidden.shape[1]
    span = seq * NZ * NY
    ctx = lax.axis_index("ctx")
    position = window[0] * span + ctx * seq + jnp.arange(seq, dtype=jnp.int32)
    inv_freq = jnp.exp(jnp.arange(HW // 2, dtype=F32) * (-2.0 * math.log(1000000.0) / HW))
    angles = position.astype(F32)[:, None] * inv_freq
    cosine, sine = jnp.cos(angles), jnp.sin(angles)
    cosine = jnp.concatenate([cosine, cosine], axis=1)
    sine = jnp.concatenate([-sine, sine], axis=1)
    info = (lengths - window * span).astype(jnp.int32)
    wT = jnp.concatenate([up_direction, up], axis=0).T
    down_out, up_out, curv_out = fisher(
        info, hidden[0], queries[0], keys[0], down.T, direction.T, up_direction, cosine, sine, wT, up
    )
    return down_out.T, up_out.T, curv_out[0, 0]


def solution(mesh):
    placed = (
        P("dp", "ctx", None),
        P("dp", "ctx", None),
        P("dp", "ctx", None),
        P(),
        P(),
        P(),
        P(),
        P("dp"),
        P("dp"),
    )
    return jax.shard_map(
        body,
        mesh=mesh,
        in_specs=placed,
        out_specs=(P("ctx", None), P(None, "ctx"), P()),
        check_vma=False,
    )
```

time: 137 us -> 129 us (0.942)
  Pallas kernels: 127 us -> 119 us
    pallas_call x2 -> x1, Pallas kernels: 127 us -> 119 us  [fisher(): pl.pallas_call(fisher_kernel, out_shape=(jax.ShapeDtypeStruct((RANK, 256)...]
    unnamed x16 -> x4, local copies, waits for them, and re-layouts: 5.81 us -> 4.68 us
where the time goes in v3:
time: 129 us
  Pallas kernels  119 us (92%)
  local copies, waits for them, and re-layouts  5.87 us (5%)
  between operations  1.97 us (2%)
  other arithmetic  1.84 us (1%)
    pallas_call x1, Pallas kernels, fisher(): pl.pallas_call(fisher_kernel, out_shape=(jax.ShapeDtypeStruct((RANK, 256)...  119 us
    unnamed x4, local copies, waits for them, and re-layouts  4.68 us

profile of v3, /device:TPU:1, one launch (start us, length us, event | category | flops | bytes accessed | tf_op | source)
XLA Modules:
  0.0 128.7 jit_solution(14731216064507978891)
XLA Ops:
  2.0 1.0 copy.13
  2.9 1.0 copy.12
  3.9 0.8 maximum_bitcast_fusion.wT
  4.6 0.3 fusion
  5.0 0.8 pad_maximum_fusion
  5.7 119.0 %shard_map.112 = (f32[64,256]{1,0:T(8,128)}, f32[16,64]{1,0:T(8,128)}, f32[8,128]{1,0:T(8,128)}) custom-call(s32[1]{0:T(128)S(6)} %sub.3.info, bf16[128,8192]{1,0:T(8,128)(2,1)} %bitcast.11, bf16[128,4096]{1,0:T(8,128)(2,1)} %bitcast.12, bf16[128,512]{1,0:T(8,128)(2,1)} %bitcast.15, bf16[64,8192]{1,0:T(8,128)(2,1)} %bitcast.13, bf16[64,8192]{1,0:T(8,128)(2,1)} %bitcast.14, ...), custom_call_target="tpu_custom_call" | custom-call | tf_op jit(solution)/shard_map/pallas_call | solution.py:520
  124.7 1.2 slice.3
  125.9 1.5 %copy.18 = f32[256,64]{0,1:T(8,128)} copy(f32[256,64]{0,1:T(8,128)} %bitcast.16) | data formatting | bytes 131072
  127.4 1.3 %copy.19 = f32[64,16]{0,1:T(8,128)} copy(f32[64,16]{0,1:T(8,128)} %bitcast.17) | data formatting | bytes 8192
  (2 shorter events, 0.0 us)

commit v4 on v3

--- a/solution.py
+++ b/solution.py
@@ -102,9 +102,9 @@
 
 
 def fisher_kernel(
-    info, hidden_any, queries_any, keys, down_any, direction_any, up_direction, cosine, sine, wT, up,
-    down_out, up_out, curv_out,
-    hidden, queries, down, direction, load_sem,
+    info, hidden_any, queries_any, keys, down_any, direction_any, up_direction, cosine, sine, up,
+    down_out, tail_out,
+    hidden, queries, down, direction, load_sem, wT,
     gath, qT, s_even, s_odd, p_even, p_odd, vT, act, grad, oacc, w_even, w_odd, curv_acc, mixed, upT,
     got_y, sum_y, got_z, part, got_core, sum_core, got_xy, ups, got_uy, sum_dy, got_dz, all_dp,
     gsend, grecv, send_sem, recv_sem,
@@ -148,7 +148,8 @@
 
     ys = [lax.rem(y + o, NY) for o in range(NY)]
     zs = [lax.rem(z + o, NZ) for o in range(NZ)]
-    cos, sin = cosine[...], sine[...]
+    cos = jnp.concatenate([cosine[...], cosine[...]], axis=1)
+    sin = jnp.concatenate([-sine[...], sine[...]], axis=1)
 
     def turn(u):
         u = u.astype(F32)
@@ -156,33 +157,39 @@
 
     for g in range(4):
         gath[1 + g, z, y] = turn(keys[:, g * HW : (g + 1) * HW]).astype(BF)
+    pl.semaphore_wait(barrier, 26)
+
+    made = []
+    sems = (gsend, grecv)
+
+    def ring_y(plan, block):
+        made.append(Flow(len(made), NY, y, plan, block, lambda to: at(z, to), sems))
+        return made[-1]
+
+    def ring_z(plan, block):
+        made.append(Flow(len(made), NZ, z, plan, block, lambda to: at(to, y), sems))
+        return made[-1]
+
+    def y_lane(head, zz, plan):
+        return ring_y(plan, lambda o, half: cut(gath.at[head, zz, o], half, 0))
+
+    def z_lane(head, yy, plan):
+        return ring_z(plan, lambda o, half: cut(gath.at[head, o, yy], half, 0))
+
+    def y_rest(head):
+        return ring_y(forward(NY), lambda o, half: cut(gath.at[head, :, o], half, 1))
+
+    first_z = z_lane(1, y, TWO8)
+    key_lanes = [y_lane(1, z, forward(NY))]
+    for flow in (first_z, key_lanes[0]):
+        flow.send(0)
     for copy in loads[:3]:
         copy.wait()
     gath[0, z, y, 0:RANK, :] = dot(down[...], hidden[...], NT).astype(BF)
     gath[0, z, y, RANK:HW, :] = dot(direction[...], hidden[...], NT).astype(BF)
-    pl.semaphore_wait(barrier, 26)
-
-    made = []
-    sems = (gsend, grecv)
-
-    def ring_y(plan, block):
-        made.append(Flow(len(made), NY, y, plan, block, lambda to: at(z, to), sems))
-        return made[-1]
-
-    def ring_z(plan, block):
-        made.append(Flow(len(made), NZ, z, plan, block, lambda to: at(to, y), sems))
-        return made[-1]
-
-    def y_lane(head, zz, plan):
-        return ring_y(plan, lambda o, half: cut(gath.at[head, zz, o], half, 0))
-
-    def z_lane(head, yy, plan):
-        return ring_z(plan, lambda o, half: cut(gath.at[head, o, yy], half, 0))
-
-    first_y, first_z = y_lane(0, z, DIRECT4), z_lane(1, y, TWO8)
+    first_y = y_lane(0, z, DIRECT4)
     act_lanes = {0: z_lane(0, y, forward(NZ))}
-    key_lanes = [y_lane(1, z, forward(NY))]
-    for flow in (first_z, key_lanes[0], first_y, act_lanes[0]):
+    for flow in (first_y, act_lanes[0]):
         flow.send(0)
 
     loads[3].wait()
@@ -194,7 +201,13 @@
             qT[i, :, h * HW : (h + 1) * HW] = jnp.transpose(turn(u) * scale).astype(BF)
         return 0
 
-    lax.fori_loop(0, qT.shape[0], rotate_queries, 0)
+    def rotate_some(k):
+        lax.fori_loop(4 * k, 4 * k + 4, rotate_queries, 0)
+
+    for g in range(4):
+        cols = slice(g * HW, (g + 1) * HW)
+        block = jnp.concatenate([up_direction[:, cols], up[:, cols]], axis=0).astype(F32)
+        wT[cols, :] = jnp.transpose(block).astype(BF)
 
     kvh = 4
     blocks = NZ * NY
@@ -219,6 +232,7 @@
         vT[g, HW : HW + 16, :] = ones
     grad[...] = jnp.zeros_like(grad)
     curv_acc[...] = jnp.zeros_like(curv_acc)
+    rotate_some(0)
 
     for slot in range(1, 5):
         new_keys, new_acts, landed = [], {}, []
@@ -243,19 +257,26 @@
         for flow in new_acts.values():
             flow.send(0)
         act_lanes.update(new_acts)
+        if slot == 1:
+            keys1_z = z_lane(2, y, TWO8)
+            keys1_z.send(0)
         if slot == 2:
-            keys2_y = y_lane(2, z, DIRECT4)
+            keys1_z.advance()
+        if slot == 3:
+            keys1_z.advance()
+            keys1_y = y_rest(2)
+            keys1_y.send(0)
+            keys2_y = y_lane(3, z, DIRECT4)
             keys2_y.send(0)
-            keys34_z = ring_z(THREE8, lambda o, half: cut(gath.at[3:5, o, y], half, 1))
-            keys34_z.send(0)
-        if slot == 3:
+        if slot == 4:
             keys2_y.receive(0)
-            keys2_z = ring_z(THREE8, lambda o, half: cut(gath.at[2, o], half, 1))
+            keys2_z = ring_z(forward(NZ), lambda o, half: cut(gath.at[3, o], half, 1))
             keys2_z.send(0)
-            keys34_z.advance()
-        if slot == 4:
-            keys2_z.advance()
-            keys34_z.advance()
+            keys3_z = z_lane(4, y, TWO8)
+            keys3_z.send(0)
+            keys3_y = y_rest(4)
+        if slot < 4:
+            rotate_some(slot)
         for oz, oy in landed:
             tangents(zs[oz], ys[oy])
     assert not key_lanes and not act_lanes
@@ -304,38 +325,41 @@
             w_bufs[odd][...] = (out * inv).astype(BF)
         return jnp.max(mx, axis=0, keepdims=True)
 
-    def y_rest(head):
-        return ring_y(forward(NY), lambda o, half: cut(gath.at[head, :, o], half, 1))
+    def pass_on(flow, step, then=None):
+        def act():
+            flow.receive(step)
+            if then is not None:
+                then[0].send(then[1])
+
+        return act
+
+    hooks = {
+        2: [pass_on(keys1_y, 0, (keys1_y, 1)), pass_on(keys2_z, 0, (keys2_z, 1))],
+        3: [pass_on(keys3_z, 0, (keys3_z, 1))],
+        4: [pass_on(keys1_y, 1), pass_on(keys2_z, 1, (keys2_z, 2))],
+        5: [pass_on(keys3_z, 1, (keys3_y, 0))],
+        6: [pass_on(keys2_z, 2, (keys2_z, 3))],
+        8: [pass_on(keys2_z, 3)],
+        9: [pass_on(keys3_y, 0, (keys3_y, 1))],
+        12: [pass_on(keys3_y, 1)],
+    }
+
+    def serve(i, odd):
+        for n, acts in hooks.items():
+            if n % 2 == odd:
+
+                @pl.when(i == n // 2)
+                def _():
+                    for act in acts:
+                        act()
 
     top = step(0, 0, True, False, False, None)
-    keys2_z.advance()
-    keys34_z.advance()
-    keys3_y, keys4_y = y_rest(3), y_rest(4)
-    keys3_y.send(0)
-    keys4_y.send(0)
     top = step(1, 1, True, True, False, top)
 
     def pair(i, top):
-        @pl.when(i == 2)
-        def _():
-            keys2_z.receive(2)
-            keys3_y.receive(0)
-            keys3_y.send(1)
-
-        @pl.when(i == 3)
-        def _():
-            keys4_y.receive(0)
-            keys4_y.send(1)
-
-        @pl.when(i == 4)
-        def _():
-            keys3_y.receive(1)
-
-        @pl.when(i == 6)
-        def _():
-            keys4_y.receive(1)
-
+        serve(i, 0)
         top = step(2 * i, 0, True, True, True, top)
+        serve(i, 1)
         return step(2 * i + 1, 1, True, True, True, top)
 
     top = lax.fori_loop(1, total // 2, pair, top)
@@ -498,22 +522,18 @@
     tail = all_dp[0, 16:32]
     for r in range(1, 8):
         tail = tail + all_dp[r, 16:32]
-    curv_sum = jnp.sum(tail[8:9])
-    count = jnp.sum(tail[9:10])
-    rescale = squared / (curv_sum + 1e-06)
     for r in range(8):
-        down_out[8 * r : 8 * r + 8, 0:HW] = all_dp[r, 0:8] * rescale
-        down_out[8 * r : 8 * r + 8, HW : 2 * HW] = all_dp[r, 8:16] * rescale
-    up_out[0:8, :] = tail[0:8, 0:RANK] * rescale
-    up_out[8:16, :] = tail[0:8, RANK:HW] * rescale
-    curv_out[...] = jnp.full((8, HW), curv_sum / count, F32)
+        down_out[8 * r : 8 * r + 8, 0:HW] = all_dp[r, 0:8]
+        down_out[8 * r : 8 * r + 8, HW : 2 * HW] = all_dp[r, 8:16]
+    tail_out[0:16, :] = tail
+    tail_out[16:24, :] = jnp.full((8, HW), squared, F32)
     for flow in made:
         flow.drain()
     for copy in sent:
         copy.wait_send()
 
 
-def fisher(info, hidden, queries, keys, down, direction, up_direction, cosine, sine, wT, up):
+def fisher(info, hidden, queries, keys, down, direction, up_direction, cosine, sine, up):
     span = NZ * NY * HW
     half = NZ // 2
     anywhere = pl.BlockSpec(memory_space=pl.ANY)
@@ -521,17 +541,17 @@
         fisher_kernel,
         out_shape=(
             jax.ShapeDtypeStruct((RANK, 256), F32),
-            jax.ShapeDtypeStruct((16, RANK), F32),
-            jax.ShapeDtypeStruct((8, HW), F32),
+            jax.ShapeDtypeStruct((24, HW), F32),
         ),
-        in_specs=[SM, anywhere, anywhere, VM, anywhere, anywhere, VM, VM, VM, VM, VM],
-        out_specs=(VM, VM, VM),
+        in_specs=[SM, anywhere, anywhere, VM, anywhere, anywhere, VM, VM, VM, VM],
+        out_specs=(VM, VM),
         scratch_shapes=[
             pltpu.VMEM(hidden.shape, BF),
             pltpu.VMEM(queries.shape, BF),
             pltpu.VMEM(down.shape, BF),
             pltpu.VMEM(direction.shape, BF),
             pltpu.SemaphoreType.DMA((4,)),
+            pltpu.VMEM((4 * HW, HW), BF),
             pltpu.VMEM((5, NZ, NY, HW, HW), BF),
             pltpu.VMEM((queries.shape[1] // ROWS, HW, ROWS), BF),
             pltpu.VMEM((span, ROWS), F32),
@@ -559,15 +579,38 @@
             pltpu.VMEM((NZ, 32, HW), F32),
             pltpu.VMEM((NZ - 1, 32, HW), F32),
             pltpu.VMEM((8, 32, HW), F32),
-            pltpu.SemaphoreType.DMA((19, 4, 4)),
-            pltpu.SemaphoreType.DMA((19, 4, 4)),
+            pltpu.SemaphoreType.DMA((20, 4, 4)),
+            pltpu.SemaphoreType.DMA((20, 4, 4)),
             pltpu.SemaphoreType.DMA((59,)),
             pltpu.SemaphoreType.DMA((59,)),
         ],
         compiler_params=pltpu.CompilerParams(
             collective_id=0, has_side_effects=True, vmem_limit_bytes=58 * 1024 * 1024
         ),
-    )(info, hidden, queries, keys, down, direction, up_direction, cosine, sine, wT, up)
+    )(info, hidden, queries, keys, down, direction, up_direction, cosine, sine, up)
+
+
+def scale_kernel(down_sum, tail, down_out, up_out, curv_out):
+    curv_sum = jnp.sum(tail[8:9, :])
+    count = jnp.sum(tail[9:10, :])
+    rescale = tail[16:17, 0:1] / (curv_sum + 1e-06)
+    down_out[...] = down_sum[...] * rescale
+    up_out[0:8, :] = tail[0:8, 0:RANK] * rescale
+    up_out[8:16, :] = tail[0:8, RANK:HW] * rescale
+    curv_out[0, 0] = curv_sum / count
+
+
+def scaled(down_sum, tail):
+    return pl.pallas_call(
+        scale_kernel,
+        out_shape=(
+            jax.ShapeDtypeStruct((RANK, 256), F32),
+            jax.ShapeDtypeStruct((16, RANK), F32),
+            jax.ShapeDtypeStruct((1, 1), F32),
+        ),
+        in_specs=[VM, VM],
+        out_specs=(VM, VM, SM),
+    )(down_sum, tail)
 
 
 def body(hidden, queries, keys, down, up, direction, up_direction, window, lengths):
@@ -578,13 +621,11 @@
     inv_freq = jnp.exp(jnp.arange(HW // 2, dtype=F32) * (-2.0 * math.log(1000000.0) / HW))
     angles = position.astype(F32)[:, None] * inv_freq
     cosine, sine = jnp.cos(angles), jnp.sin(angles)
-    cosine = jnp.concatenate([cosine, cosine], axis=1)
-    sine = jnp.concatenate([-sine, sine], axis=1)
     info = (lengths - window * span).astype(jnp.int32)
-    wT = jnp.concatenate([up_direction, up], axis=0).T
-    down_out, up_out, curv_out = fisher(
-        info, hidden[0], queries[0], keys[0], down.T, direction.T, up_direction, cosine, sine, wT, up
+    down_sum, tail = fisher(
+        info, hidden[0], queries[0], keys[0], down.T, direction.T, up_direction, cosine, sine, up
     )
+    down_out, up_out, curv_out = scaled(down_sum, tail)
     return down_out.T, up_out.T, curv_out[0, 0]
 
 

time: 129 us -> 120 us (0.930)
  local copies, waits for them, and re-layouts: 5.87 us -> 0 us
  Pallas kernels: 119 us -> 117 us
    unnamed x4 -> x0, local copies, waits for them, and re-layouts: 4.68 us -> none
    pallas_call x1, Pallas kernels: 119 us -> 115 us  [fisher(): pl.pallas_call(fisher_kernel, out_shape=(jax.ShapeDtypeStruct((RANK, 256)...]
    pallas_call x0 -> x1, Pallas kernels: none -> 1.68 us  [scaled(): pl.pallas_call(scale_kernel, out_shape=(jax.ShapeDtypeStruct((RANK, 256),...]
where the time goes in v4:
time: 120 us
  Pallas kernels  117 us (98%)
  between operations  2.11 us (2%)
    pallas_call x1, Pallas kernels, fisher(): pl.pallas_call(fisher_kernel, out_shape=(jax.ShapeDtypeStruct((RANK, 256)...  115 us

profile of v4, /device:TPU:1, one launch (start us, length us, event | category | flops | bytes accessed | tf_op | source)
XLA Modules:
  0.0 119.6 jit_solution(13215143594601821415)
XLA Ops:
  2.0 0.9 multiply_sine_fusion
  2.9 114.9 %shard_map.112 = (f32[64,256]{1,0:T(8,128)}, f32[24,128]{1,0:T(8,128)}) custom-call(s32[1]{0:T(128)S(6)} %sub.3.info, bf16[128,8192]{1,0:T(8,128)(2,1)} %bitcast.9, bf16[128,4096]{1,0:T(8,128)(2,1)} %bitcast.10, bf16[128,512]{1,0:T(8,128)(2,1)} %bitcast.13, bf16[64,8192]{1,0:T(8,128)(2,1)} %bitcast.11, bf16[64,8192]{1,0:T(8,128)(2,1)} %bitcast.12, ...), custom_call_target="tpu_custom_call" | custom-call | tf_op jit(solution)/shard_map/pallas_call | solution.py:540
  117.8 1.7 %shard_map.113 = (f32[64,256]{1,0:T(8,128)}, f32[16,64]{1,0:T(8,128)}, f32[1,1]{1,0:T(1,128)}) custom-call(f32[64,256]{1,0:T(8,128)} %get-tuple-element.8.down_sum, f32[24,128]{1,0:T(8,128)} %get-tuple-element.9.tail), custom_call_target="tpu_custom_call" | custom-call | tf_op jit(solution)/shard_map/pallas_call | solution.py:604
  (2 shorter events, 0.0 us)

commit v5 on v4

--- a/solution.py
+++ b/solution.py
@@ -188,9 +188,7 @@
     gath[0, z, y, 0:RANK, :] = dot(down[...], hidden[...], NT).astype(BF)
     gath[0, z, y, RANK:HW, :] = dot(direction[...], hidden[...], NT).astype(BF)
     first_y = y_lane(0, z, DIRECT4)
-    act_lanes = {0: z_lane(0, y, forward(NZ))}
-    for flow in (first_y, act_lanes[0]):
-        flow.send(0)
+    first_y.send(0)
 
     loads[3].wait()
     scale = math.log2(math.e) / math.sqrt(HW)
@@ -233,53 +231,6 @@
     grad[...] = jnp.zeros_like(grad)
     curv_acc[...] = jnp.zeros_like(curv_acc)
     rotate_some(0)
-
-    for slot in range(1, 5):
-        new_keys, new_acts, landed = [], {}, []
-        if slot <= 2:
-            came, _ = first_z.advance()
-            new_keys = [y_lane(1, zs[o], forward(NY) if slot == 1 else DIRECT4) for o in came]
-        for flow in list(key_lanes):
-            if flow.advance()[1]:
-                key_lanes.remove(flow)
-        for flow in new_keys:
-            flow.send(0)
-        key_lanes += new_keys
-        if slot == 1:
-            came, _ = first_y.advance()
-            new_acts = {o: z_lane(0, ys[o], THREE8) for o in came}
-            landed += [(0, o) for o in came]
-        for o, flow in list(act_lanes.items()):
-            came, end = flow.advance()
-            landed += [(oz, o) for oz in came]
-            if end:
-                del act_lanes[o]
-        for flow in new_acts.values():
-            flow.send(0)
-        act_lanes.update(new_acts)
-        if slot == 1:
-            keys1_z = z_lane(2, y, TWO8)
-            keys1_z.send(0)
-        if slot == 2:
-            keys1_z.advance()
-        if slot == 3:
-            keys1_z.advance()
-            keys1_y = y_rest(2)
-            keys1_y.send(0)
-            keys2_y = y_lane(3, z, DIRECT4)
-            keys2_y.send(0)
-        if slot == 4:
-            keys2_y.receive(0)
-            keys2_z = ring_z(forward(NZ), lambda o, half: cut(gath.at[3, o], half, 1))
-            keys2_z.send(0)
-            keys3_z = z_lane(4, y, TWO8)
-            keys3_z.send(0)
-            keys3_y = y_rest(4)
-        if slot < 4:
-            rotate_some(slot)
-        for oz, oy in landed:
-            tangents(zs[oz], ys[oy])
-    assert not key_lanes and not act_lanes
 
     s_bufs, p_bufs, w_bufs = (s_even, s_odd), (p_even, p_odd), (w_even, w_odd)
     qpos = me * HW + lax.rem(lax.broadcasted_iota(jnp.int32, (1, ROWS), 1), HW)
@@ -325,6 +276,50 @@
             w_bufs[odd][...] = (out * inv).astype(BF)
         return jnp.max(mx, axis=0, keepdims=True)
 
+    for slot in range(1, 5):
+        new_keys, landed = [], []
+        if slot <= 2:
+            came, _ = first_z.advance()
+            new_keys = [y_lane(1, zs[o], forward(NY) if slot == 1 else DIRECT4) for o in came]
+        for flow in list(key_lanes):
+            if flow.advance()[1]:
+                key_lanes.remove(flow)
+        for flow in new_keys:
+            flow.send(0)
+        key_lanes += new_keys
+        if slot == 1:
+            came, _ = first_y.advance()
+            landed += [(0, o) for o in came]
+            acts = ring_z(THREE8, lambda o, half: cut(gath.at[0, o], half, 1))
+            acts.send(0)
+        else:
+            came, _ = acts.advance()
+            landed += [(oz, oy) for oz in came for oy in range(NY)]
+        if slot == 1:
+            keys1_z = z_lane(2, y, TWO8)
+            keys1_z.send(0)
+        if slot == 2:
+            keys1_z.advance()
+        if slot == 3:
+            keys1_z.advance()
+            keys1_y = y_rest(2)
+            keys1_y.send(0)
+            keys2_y = y_lane(3, z, DIRECT4)
+            keys2_y.send(0)
+        if slot == 4:
+            keys2_y.receive(0)
+            keys2_z = ring_z(forward(NZ), lambda o, half: cut(gath.at[3, o], half, 1))
+            keys2_z.send(0)
+            keys3_z = z_lane(4, y, TWO8)
+            keys3_z.send(0)
+            keys3_y = y_rest(4)
+        if slot < 4:
+            rotate_some(slot)
+        for oz, oy in landed:
+            tangents(zs[oz], ys[oy])
+        if slot == 3:
+            top = step(0, 0, True, False, False, None)
+
     def pass_on(flow, step, then=None):
         def act():
             flow.receive(step)
@@ -353,7 +348,6 @@
                     for act in acts:
                         act()
 
-    top = step(0, 0, True, False, False, None)
     top = step(1, 1, True, True, False, top)
 
     def pair(i, top):
@@ -579,8 +573,8 @@
             pltpu.VMEM((NZ, 32, HW), F32),
             pltpu.VMEM((NZ - 1, 32, HW), F32),
             pltpu.VMEM((8, 32, HW), F32),
-            pltpu.SemaphoreType.DMA((20, 4, 4)),
-            pltpu.SemaphoreType.DMA((20, 4, 4)),
+            pltpu.SemaphoreType.DMA((17, 4, 4)),
+            pltpu.SemaphoreType.DMA((17, 4, 4)),
             pltpu.SemaphoreType.DMA((59,)),
             pltpu.SemaphoreType.DMA((59,)),
         ],

time: 120 us -> 121 us (level)
  no operation moved by 1% of the time
where the time goes in v5:
time: 121 us; the launch traced here: 120 us
  Pallas kernels  117 us (97%)
  between operations  2.11 us (2%)
    pallas_call x1, Pallas kernels, fisher(): pl.pallas_call(fisher_kernel, out_shape=(jax.ShapeDtypeStruct((RANK, 256)...  116 us

profile of v5, /device:TPU:1, one launch (start us, length us, event | category | flops | bytes accessed | tf_op | source)
XLA Modules:
  0.0 120.5 jit_solution(2593569979319167180)
XLA Ops:
  2.0 0.9 multiply_sine_fusion
  2.9 115.7 %shard_map.112 = (f32[64,256]{1,0:T(8,128)}, f32[24,128]{1,0:T(8,128)}) custom-call(s32[1]{0:T(128)S(6)} %sub.3.info, bf16[128,8192]{1,0:T(8,128)(2,1)} %bitcast.9, bf16[128,4096]{1,0:T(8,128)(2,1)} %bitcast.10, bf16[128,512]{1,0:T(8,128)(2,1)} %bitcast.13, bf16[64,8192]{1,0:T(8,128)(2,1)} %bitcast.11, bf16[64,8192]{1,0:T(8,128)(2,1)} %bitcast.12, ...), custom_call_target="tpu_custom_call" | custom-call | tf_op jit(solution)/shard_map/pallas_call | solution.py:534
  118.6 1.7 %shard_map.113 = (f32[64,256]{1,0:T(8,128)}, f32[16,64]{1,0:T(8,128)}, f32[1,1]{1,0:T(1,128)}) custom-call(f32[64,256]{1,0:T(8,128)} %get-tuple-element.8.down_sum, f32[24,128]{1,0:T(8,128)} %get-tuple-element.9.tail), custom_call_target="tpu_custom_call" | custom-call | tf_op jit(solution)/shard_map/pallas_call | solution.py:598
  (2 shorter events, 0.0 us)

commit v6 on v5

--- a/solution.py
+++ b/solution.py
@@ -95,16 +95,16 @@
                 self.copy(step, k, False).wait_send()
 
 
-def cut(ref, half, axis):
+def cut(ref, half, axis, rows=64):
     if half is None:
         return ref
-    return ref.at[(slice(None),) * axis + (pl.ds(half * 64, 64),)]
+    return ref.at[(slice(None),) * axis + (pl.ds(half * rows, rows),)]
 
 
 def fisher_kernel(
     info, hidden_any, queries_any, keys, down_any, direction_any, up_direction, cosine, sine, up,
     down_out, tail_out,
-    hidden, queries, down, direction, load_sem, wT,
+    hidden, queries, down, direction, load_sem, wT, ranks,
     gath, qT, s_even, s_odd, p_even, p_odd, vT, act, grad, oacc, w_even, w_odd, curv_acc, mixed, upT,
     got_y, sum_y, got_z, part, got_core, sum_core, got_xy, ups, got_uy, sum_dy, got_dz, all_dp,
     gsend, grecv, send_sem, recv_sem,
@@ -156,7 +156,7 @@
         return u * cos + pltpu.roll(u, HW // 2, 1) * sin
 
     for g in range(4):
-        gath[1 + g, z, y] = turn(keys[:, g * HW : (g + 1) * HW]).astype(BF)
+        gath[g, z, y] = turn(keys[:, g * HW : (g + 1) * HW]).astype(BF)
     pl.semaphore_wait(barrier, 26)
 
     made = []
@@ -179,16 +179,18 @@
     def y_rest(head):
         return ring_y(forward(NY), lambda o, half: cut(gath.at[head, :, o], half, 1))
 
-    first_z = z_lane(1, y, TWO8)
-    key_lanes = [y_lane(1, z, forward(NY))]
+    first_z = z_lane(0, y, TWO8)
+    key_lanes = [y_lane(0, z, forward(NY))]
     for flow in (first_z, key_lanes[0]):
         flow.send(0)
     for copy in loads[:3]:
         copy.wait()
-    gath[0, z, y, 0:RANK, :] = dot(down[...], hidden[...], NT).astype(BF)
-    gath[0, z, y, RANK:HW, :] = dot(direction[...], hidden[...], NT).astype(BF)
-    first_y = y_lane(0, z, DIRECT4)
-    first_y.send(0)
+    ranks[0, z, y] = dot(down[...], hidden[...], NT).astype(BF)
+    ranks[1, z, y] = dot(direction[...], hidden[...], NT).astype(BF)
+    first_y = ring_y(DIRECT4, lambda o, half: ranks.at[0, z, o])
+    tans_z = ring_z(TWO8, lambda o, half: cut(ranks.at[1, o, y], half, 0, 32))
+    for flow in (first_y, tans_z):
+        flow.send(0)
 
     loads[3].wait()
     scale = math.log2(math.e) / math.sqrt(HW)
@@ -219,12 +221,12 @@
 
     def tangents(zz, yy):
         cols = pl.ds(pl.multiple_of((zz * NY + yy) * HW, HW), HW)
-        vv = dot(wT[...], gath[0, zz, yy]).astype(BF)
+        block = jnp.concatenate([ranks[0, zz, yy], ranks[1, zz, yy]], axis=0)
+        vv = dot(wT[...], block).astype(BF)
         for g in range(kvh):
             vT[g, 0:HW, cols] = vv[g * HW : (g + 1) * HW]
-        act[:, cols] = gath[0, zz, yy, 0:RANK, :]
-
-    tangents(z, y)
+        act[:, cols] = ranks[0, zz, yy]
+
     ones = jnp.where(lax.broadcasted_iota(jnp.int32, (16, span), 0) == 0, 1.0, 0.0).astype(BF)
     for g in range(kvh):
         vT[g, HW : HW + 16, :] = ones
@@ -252,7 +254,7 @@
                     )
                 if score:
                     b = u * (SUB // HW)
-                    kc = gath[1 + i // per_g, j * zper + b // NY, b % NY : b % NY + SUB // HW].reshape(SUB, HW)
+                    kc = gath[i // per_g, j * zper + b // NY, b % NY : b % NY + SUB // HW].reshape(SUB, HW)
                     s = dot(kc, q)
                     kpos = us + lax.broadcasted_iota(jnp.int32, (SUB, ROWS), 0)
                     s = jnp.where(kpos <= qpos, s, -1e30)
@@ -277,10 +279,10 @@
         return jnp.max(mx, axis=0, keepdims=True)
 
     for slot in range(1, 5):
-        new_keys, landed = [], []
+        new_keys = []
         if slot <= 2:
             came, _ = first_z.advance()
-            new_keys = [y_lane(1, zs[o], forward(NY) if slot == 1 else DIRECT4) for o in came]
+            new_keys = [y_lane(0, zs[o], forward(NY) if slot == 1 else DIRECT4) for o in came]
         for flow in list(key_lanes):
             if flow.advance()[1]:
                 key_lanes.remove(flow)
@@ -288,31 +290,41 @@
             flow.send(0)
         key_lanes += new_keys
         if slot == 1:
-            came, _ = first_y.advance()
-            landed += [(0, o) for o in came]
-            acts = ring_z(THREE8, lambda o, half: cut(gath.at[0, o], half, 1))
+            first_y.advance()
+            acts = ring_z(THREE8, lambda o, half: cut(ranks.at[0, o], half, 1, 32))
             acts.send(0)
+            tans_z.advance()
         else:
-            came, _ = acts.advance()
-            landed += [(oz, oy) for oz in came for oy in range(NY)]
+            acts.advance()
+        if slot == 2:
+            tans_z.advance()
+            tans_y = ring_y(DIRECT4, lambda o, half: ranks.at[1, :, o])
+            tans_y.send(0)
+        if slot == 3:
+            tans_y.advance()
+        acts_by = (1, 2, 3, 4, 4, 4, 3, 2)
+        tans_by = (2, 3, 3, 3)
+        landed = [
+            (oz, oy) for oz in range(NZ) for oy in range(NY) if max(acts_by[oz], tans_by[oy]) == slot
+        ]
         if slot == 1:
-            keys1_z = z_lane(2, y, TWO8)
+            keys1_z = z_lane(1, y, TWO8)
             keys1_z.send(0)
         if slot == 2:
             keys1_z.advance()
         if slot == 3:
             keys1_z.advance()
-            keys1_y = y_rest(2)
+            keys1_y = y_rest(1)
             keys1_y.send(0)
-            keys2_y = y_lane(3, z, DIRECT4)
+            keys2_y = y_lane(2, z, DIRECT4)
             keys2_y.send(0)
         if slot == 4:
             keys2_y.receive(0)
-            keys2_z = ring_z(forward(NZ), lambda o, half: cut(gath.at[3, o], half, 1))
+            keys2_z = ring_z(forward(NZ), lambda o, half: cut(gath.at[2, o], half, 1))
             keys2_z.send(0)
-            keys3_z = z_lane(4, y, TWO8)
+            keys3_z = z_lane(3, y, TWO8)
             keys3_z.send(0)
-            keys3_y = y_rest(4)
+            keys3_y = y_rest(3)
         if slot < 4:
             rotate_some(slot)
         for oz, oy in landed:
@@ -546,7 +558,8 @@
             pltpu.VMEM(direction.shape, BF),
             pltpu.SemaphoreType.DMA((4,)),
             pltpu.VMEM((4 * HW, HW), BF),
-            pltpu.VMEM((5, NZ, NY, HW, HW), BF),
+            pltpu.VMEM((2, NZ, NY, RANK, HW), BF),
+            pltpu.VMEM((4, NZ, NY, HW, HW), BF),
             pltpu.VMEM((queries.shape[1] // ROWS, HW, ROWS), BF),
             pltpu.VMEM((span, ROWS), F32),
             pltpu.VMEM((span, ROWS), F32),
@@ -573,8 +586,8 @@
             pltpu.VMEM((NZ, 32, HW), F32),
             pltpu.VMEM((NZ - 1, 32, HW), F32),
             pltpu.VMEM((8, 32, HW), F32),
-            pltpu.SemaphoreType.DMA((17, 4, 4)),
-            pltpu.SemaphoreType.DMA((17, 4, 4)),
+            pltpu.SemaphoreType.DMA((19, 4, 4)),
+            pltpu.SemaphoreType.DMA((19, 4, 4)),
             pltpu.SemaphoreType.DMA((59,)),
             pltpu.SemaphoreType.DMA((59,)),
         ],

time: 121 us -> 126 us (1.041)
  Pallas kernels: 117 us -> 122 us
    pallas_call x1, Pallas kernels: 116 us -> 121 us  [fisher(): pl.pallas_call(fisher_kernel, out_shape=(jax.ShapeDtypeStruct((RANK, 256)...]
where the time goes in v6:
time: 126 us; the launch traced here: 125 us
  Pallas kernels  122 us (97%)
  between operations  2.11 us (2%)
    pallas_call x1, Pallas kernels, fisher(): pl.pallas_call(fisher_kernel, out_shape=(jax.ShapeDtypeStruct((RANK, 256)...  121 us

profile of v6, /device:TPU:1, one launch (start us, length us, event | category | flops | bytes accessed | tf_op | source)
XLA Modules:
  0.0 125.3 jit_solution(481965645445729640)
XLA Ops:
  2.0 0.9 multiply_sine_fusion
  2.9 120.6 %shard_map.112 = (f32[64,256]{1,0:T(8,128)}, f32[24,128]{1,0:T(8,128)}) custom-call(s32[1]{0:T(128)S(6)} %sub.3.info, bf16[128,8192]{1,0:T(8,128)(2,1)} %bitcast.9, bf16[128,4096]{1,0:T(8,128)(2,1)} %bitcast.10, bf16[128,512]{1,0:T(8,128)(2,1)} %bitcast.13, bf16[64,8192]{1,0:T(8,128)(2,1)} %bitcast.11, bf16[64,8192]{1,0:T(8,128)(2,1)} %bitcast.12, ...), custom_call_target="tpu_custom_call" | custom-call | tf_op jit(solution)/shard_map/pallas_call | solution.py:546
  123.5 1.7 %shard_map.113 = (f32[64,256]{1,0:T(8,128)}, f32[16,64]{1,0:T(8,128)}, f32[1,1]{1,0:T(1,128)}) custom-call(f32[64,256]{1,0:T(8,128)} %get-tuple-element.8.down_sum, f32[24,128]{1,0:T(8,128)} %get-tuple-element.9.tail), custom_call_target="tpu_custom_call" | custom-call | tf_op jit(solution)/shard_map/pallas_call | solution.py:611
  (2 shorter events, 0.0 us)

commit v7 on v5

--- a/solution.py
+++ b/solution.py
@@ -188,7 +188,9 @@
     gath[0, z, y, 0:RANK, :] = dot(down[...], hidden[...], NT).astype(BF)
     gath[0, z, y, RANK:HW, :] = dot(direction[...], hidden[...], NT).astype(BF)
     first_y = y_lane(0, z, DIRECT4)
-    first_y.send(0)
+    act_lanes = {0: z_lane(0, y, forward(NZ))}
+    for flow in (first_y, act_lanes[0]):
+        flow.send(0)
 
     loads[3].wait()
     scale = math.log2(math.e) / math.sqrt(HW)
@@ -277,24 +279,28 @@
         return jnp.max(mx, axis=0, keepdims=True)
 
     for slot in range(1, 5):
-        new_keys, landed = [], []
+        new_keys, new_acts, landed = [], {}, []
         if slot <= 2:
             came, _ = first_z.advance()
             new_keys = [y_lane(1, zs[o], forward(NY) if slot == 1 else DIRECT4) for o in came]
+            for flow in new_keys:
+                flow.send(0)
+        if slot == 1:
+            came, _ = first_y.advance()
+            new_acts = {o: z_lane(0, ys[o], THREE8) for o in came}
+            landed += [(0, o) for o in came]
+        for o, flow in list(act_lanes.items()):
+            came, end = flow.advance()
+            landed += [(oz, o) for oz in came]
+            if end:
+                del act_lanes[o]
+        for flow in new_acts.values():
+            flow.send(0)
+        act_lanes.update(new_acts)
         for flow in list(key_lanes):
             if flow.advance()[1]:
                 key_lanes.remove(flow)
-        for flow in new_keys:
-            flow.send(0)
         key_lanes += new_keys
-        if slot == 1:
-            came, _ = first_y.advance()
-            landed += [(0, o) for o in came]
-            acts = ring_z(THREE8, lambda o, half: cut(gath.at[0, o], half, 1))
-            acts.send(0)
-        else:
-            came, _ = acts.advance()
-            landed += [(oz, oy) for oz in came for oy in range(NY)]
         if slot == 1:
             keys1_z = z_lane(2, y, TWO8)
             keys1_z.send(0)
@@ -573,8 +579,8 @@
             pltpu.VMEM((NZ, 32, HW), F32),
             pltpu.VMEM((NZ - 1, 32, HW), F32),
             pltpu.VMEM((8, 32, HW), F32),
-            pltpu.SemaphoreType.DMA((17, 4, 4)),
-            pltpu.SemaphoreType.DMA((17, 4, 4)),
+            pltpu.SemaphoreType.DMA((20, 4, 4)),
+            pltpu.SemaphoreType.DMA((20, 4, 4)),
             pltpu.SemaphoreType.DMA((59,)),
             pltpu.SemaphoreType.DMA((59,)),
         ],

time: 121 us -> 121 us (level)
  no operation moved by 1% of the time
where the time goes in v7:
time: 121 us
  Pallas kernels  118 us (98%)
  between operations  2.11 us (2%)
    pallas_call x1, Pallas kernels, fisher(): pl.pallas_call(fisher_kernel, out_shape=(jax.ShapeDtypeStruct((RANK, 256)...  116 us

profile of v7, /device:TPU:1, one launch (start us, length us, event | category | flops | bytes accessed | tf_op | source)
XLA Modules:
  0.0 120.9 jit_solution(7523808744824945612)
XLA Ops:
  2.0 0.9 multiply_sine_fusion
  2.9 116.2 %shard_map.112 = (f32[64,256]{1,0:T(8,128)}, f32[24,128]{1,0:T(8,128)}) custom-call(s32[1]{0:T(128)S(6)} %sub.3.info, bf16[128,8192]{1,0:T(8,128)(2,1)} %bitcast.9, bf16[128,4096]{1,0:T(8,128)(2,1)} %bitcast.10, bf16[128,512]{1,0:T(8,128)(2,1)} %bitcast.13, bf16[64,8192]{1,0:T(8,128)(2,1)} %bitcast.11, bf16[64,8192]{1,0:T(8,128)(2,1)} %bitcast.12, ...), custom_call_target="tpu_custom_call" | custom-call | tf_op jit(solution)/shard_map/pallas_call | solution.py:540
  119.1 1.7 %shard_map.113 = (f32[64,256]{1,0:T(8,128)}, f32[16,64]{1,0:T(8,128)}, f32[1,1]{1,0:T(1,128)}) custom-call(f32[64,256]{1,0:T(8,128)} %get-tuple-element.8.down_sum, f32[24,128]{1,0:T(8,128)} %get-tuple-element.9.tail), custom_call_target="tpu_custom_call" | custom-call | tf_op jit(solution)/shard_map/pallas_call | solution.py:604
  (2 shorter events, 0.0 us)
